TPU v7x, 256 devices: a whole 4x4x8 slice. The times are simulated.
256 devices in a mesh: dp: 16 (over z_lo, x), sp: 16 (over z_hi, y, core).
Axes of the slice: x: 4, y: 4, z: 8 (z_hi: 2, z_lo: 4; z = z_hi * 4 + z_lo), core: 2. Of those that a mesh axis runs over, the one named last changes fastest.
Arguments:
- queries: bfloat16 [2, 16, 2048, 2048], P(None, 'dp', 'sp'), may hold values from -40 to 40
- dout: bfloat16 [2, 16, 2048, 2048], P(None, 'dp', 'sp'), may hold values from -16 to 16
- keys: bfloat16 [16, 2048, 1024], P('dp', 'sp'), may hold values from -40 to 40
- values: bfloat16 [16, 2048, 1024], P('dp', 'sp'), may hold values from -6 to 6
- gain: float32 [2, 128], replicated, may hold values from 0.5 to 2
- segments: int32 [16, 2048], P('dp', 'sp'), may hold values from 0 to 7, never falling along the last dimension, each value on 1 to 1024 neighbouring positions
Outputs:
- dqueries: bfloat16 [2, 16, 2048, 2048], P(None, 'dp', 'sp')
- dkeys: bfloat16 [16, 2048, 1024], P('dp', 'sp')
- dvalues: bfloat16 [16, 2048, 1024], P('dp', 'sp')
- dgain: float32 [2, 128], replicated
All inputs are finite; a program needn't handle non-finite values.
Results may differ from a plain program's by a relative error of at most 0.01.
The roundings to bfloat16 on the way count: a program that leaves them out, or rounds other values in their place, can miss the bound.
Values may be sent and summed in bfloat16 or wider, within the bound.
No kernel may reach another device: no remote copies, remote signals or barrier semaphores. Data moves between devices by JAX's collectives and lax.ppermute only.
A program may use at most 64 MiB of HBM per device.

v0:
```python
import math

import jax
import jax.numpy as jnp
from jax import lax
from jax.sharding import PartitionSpec as P


def block_grads(query_blk, dout_blk, seg_q, pos_q, key_h, value_h, seg_k, pos_k, gain_l, scale):
    qf = query_blk.astype(jnp.float32)
    inv = lax.rsqrt(jnp.mean(qf * qf, axis=-1, keepdims=True) + 1e-06)
    qhat = qf * inv
    normed = (qhat * gain_l).astype(jnp.bfloat16)
    scores = jnp.einsum("bkgd,skd->kgbs", normed, key_h, preferred_element_type=jnp.float32) * scale
    allowed = (seg_q[:, None] == seg_k[None, :]) & (pos_k[None, :] <= pos_q[:, None])
    scores = jnp.where(allowed, scores, -1e30)
    top = jnp.max(scores, axis=-1, keepdims=True)
    expo = jnp.exp(scores - top)
    prob = expo / jnp.sum(expo, axis=-1, keepdims=True)
    dprob = jnp.einsum("bkgd,skd->kgbs", dout_blk, value_h, preferred_element_type=jnp.float32)
    delta = jnp.sum(prob * dprob, axis=-1, keepdims=True)
    dscore = (prob * (dprob - delta) * scale).astype(jnp.bfloat16)
    prob16 = prob.astype(jnp.bfloat16)
    dvalue = jnp.einsum("kgbs,bkgd->skd", prob16, dout_blk, preferred_element_type=jnp.float32)
    dkey = jnp.einsum("kgbs,bkgd->skd", dscore, normed, preferred_element_type=jnp.float32)
    dnorm = jnp.einsum("kgbs,skd->bkgd", dscore, key_h, preferred_element_type=jnp.float32)
    dgain = jnp.sum(dnorm * qhat, axis=(0, 1, 2))
    scaled = dnorm * gain_l
    dquery = inv * (scaled - qhat * jnp.mean(scaled * qhat, axis=-1, keepdims=True))
    return (dquery.astype(jnp.bfloat16), dkey, dvalue, dgain)


def on_device(queries, dout, keys, values, gain, segments):
    layers = queries.shape[0]
    tok_rows = queries.shape[2]
    head_dim = gain.shape[1]
    heads = queries.shape[3] // head_dim
    kv_heads = keys.shape[2] // head_dim
    parts = lax.axis_size("sp")
    repeat = max(1, parts // kv_heads)
    length = tok_rows * parts
    q_local = heads // parts
    kv_local = kv_heads * repeat // parts
    group = q_local // kv_local
    block = min(512, length)
    count = length // block
    scale = 1.0 / math.sqrt(head_dim)
    seg_all = lax.all_gather(segments, "sp", axis=1, tiled=True)[0]
    positions = jnp.arange(length, dtype=jnp.int32)
    key_heads = jnp.repeat(keys[0].reshape(tok_rows, kv_heads, head_dim), repeat, axis=1)
    value_heads = jnp.repeat(values[0].reshape(tok_rows, kv_heads, head_dim), repeat, axis=1)
    key_loc, value_loc = (
        lax.all_to_all(key_heads, "sp", split_axis=1, concat_axis=0, tiled=True),
        lax.all_to_all(value_heads, "sp", split_axis=1, concat_axis=0, tiled=True),
    )
    query_heads = queries[:, 0].reshape(layers, tok_rows, heads, head_dim)
    dout_heads = dout[:, 0].reshape(layers, tok_rows, heads, head_dim)
    dkey_total = jnp.zeros((length, kv_local, head_dim), jnp.float32)
    dvalue_total = jnp.zeros((length, kv_local, head_dim), jnp.float32)
    grad_list = []
    gain_list = []
    for layer in range(layers):
        query_l, dout_l = (
            lax.all_to_all(query_heads[layer], "sp", split_axis=1, concat_axis=0, tiled=True),
            lax.all_to_all(dout_heads[layer], "sp", split_axis=1, concat_axis=0, tiled=True),
        )
        gain_l = gain[layer]
        query_b = query_l.reshape(count, block, kv_local, group, head_dim)
        dout_b = dout_l.reshape(count, block, kv_local, group, head_dim)
        seg_b = seg_all.reshape(count, block)
        pos_b = positions.reshape(count, block)

        def step(carry, xs):
            dk_acc, dv_acc, dg_acc = carry
            dq, dk, dv, dg = block_grads(
                xs[0], xs[1], xs[2], xs[3], key_loc, value_loc, seg_all, positions, gain_l, scale
            )
            return ((dk_acc + dk, dv_acc + dv, dg_acc + dg), dq)

        init = (
            jnp.zeros((length, kv_local, head_dim), jnp.float32),
            jnp.zeros((length, kv_local, head_dim), jnp.float32),
            jnp.zeros((head_dim,), jnp.float32),
        )
        (dk_l, dv_l, dg_l), dq_l = lax.scan(step, init, (query_b, dout_b, seg_b, pos_b))
        dq_l, dk_l, dv_l, dg_l = (dq_l.reshape(length, q_local, head_dim), dk_l, dv_l, dg_l)
        dkey_total = dkey_total + dk_l
        dvalue_total = dvalue_total + dv_l
        gain_list.append(dg_l)
        grad_list.append(lax.all_to_all(dq_l, "sp", split_axis=0, concat_axis=1, tiled=True))
    grad_tok = jnp.stack(grad_list)
    dqueries = grad_tok.reshape(layers, 1, tok_rows, heads * head_dim)
    dkey_back, dvalue_back = (
        lax.all_to_all(
            dkey_total.astype(jnp.bfloat16), "sp", split_axis=0, concat_axis=1, tiled=True
        ),
        lax.all_to_all(
            dvalue_total.astype(jnp.bfloat16), "sp", split_axis=0, concat_axis=1, tiled=True
        ),
    )
    dkeys = (
        jnp.sum(dkey_back.astype(jnp.float32).reshape(tok_rows, kv_heads, repeat, head_dim), axis=2)
        .astype(jnp.bfloat16)
        .reshape(1, tok_rows, kv_heads * head_dim)
    )
    dvalues = (
        jnp.sum(
            dvalue_back.astype(jnp.float32).reshape(tok_rows, kv_heads, repeat, head_dim), axis=2
        )
        .astype(jnp.bfloat16)
        .reshape(1, tok_rows, kv_heads * head_dim)
    )
    dgain = lax.psum(jnp.stack(gain_list), ("dp", "sp"))
    return (dqueries, dkeys, dvalues, dgain)


def solution(mesh):
    return jax.shard_map(
        on_device,
        mesh=mesh,
        in_specs=(
            P(None, "dp", "sp", None),
            P(None, "dp", "sp", None),
            P("dp", "sp", None),
            P("dp", "sp", None),
            P(),
            P("dp", "sp"),
        ),
        out_specs=(P(None, "dp", "sp", None), P("dp", "sp", None), P("dp", "sp", None), P()),
        check_vma=False,
    )
```

profile of v0, /device:TPU:1, one launch (start us, length us, event | category | flops | bytes accessed | tf_op | source)
XLA Modules:
  0.0 462.7 jit_solution(2416870589302216791)
XLA Ops:
  2.9 12.6 %all-to-all-start.2 = ((bf16[128,16,128]{0,2,1:T(8,128)(2,1)}), bf16[128,16,128]{0,2,1:T(8,128)(2,1)S(1)}, u32[]{:S(2)}, u32[]{:S(2)}) async-start(bf16[128,16,128]{0,2,1:T(8,128)(2,1)} %bitcast.7), calls=%async_computation.2 | async-start | bytes 1048576 | tf_op jit(solution)/shard_map/all_to_all | solution.py:65
  17.9 12.6 %all-to-all-done.2 = bf16[128,16,128]{0,2,1:T(8,128)(2,1)S(1)} async-done(((bf16[128,16,128]{0,2,1:T(8,128)(2,1)}), bf16[128,16,128]{0,2,1:T(8,128)(2,1)S(1)}, u32[]{:S(2)}, u32[]{:S(2)}) %all-to-all-start.2) | async-done | bytes 524320 | tf_op jit(solution)/shard_map/all_to_all | solution.py:65
  30.6 5.0 %all-to-all-start = ((bf16[128,16,128]{2,0,1:T(8,128)(2,1)}), bf16[128,16,128]{2,0,1:T(8,128)(2,1)}, u32[]{:S(2)}, u32[]{:S(2)}) async-start(bf16[128,16,128]{2,0,1:T(8,128)(2,1)} %copy.79), calls=%async_computation | async-start | bytes 1048576 | tf_op jit(solution)/shard_map/all_to_all | solution.py:64
  35.7 13.9 %all-to-all-done = bf16[128,16,128]{2,0,1:T(8,128)(2,1)} async-done(((bf16[128,16,128]{2,0,1:T(8,128)(2,1)}), bf16[128,16,128]{2,0,1:T(8,128)(2,1)}, u32[]{:S(2)}, u32[]{:S(2)}) %all-to-all-start) | async-done | bytes 524320 | tf_op jit(solution)/shard_map/all_to_all | solution.py:64
  50.5 8.1 %all-to-all-start.3 = ((bf16[128,16,128]{2,0,1:T(8,128)(2,1)}), bf16[128,16,128]{2,0,1:T(8,128)(2,1)}, u32[]{:S(2)}, u32[]{:S(2)}) async-start(bf16[128,16,128]{2,0,1:T(8,128)(2,1)} %bitcast.12), calls=%async_computation.3 | async-start | bytes 1048576 | tf_op jit(solution)/shard_map/all_to_all | solution.py:54
  58.7 13.8 %all-to-all-done.3 = bf16[128,16,128]{2,0,1:T(8,128)(2,1)} async-done(((bf16[128,16,128]{2,0,1:T(8,128)(2,1)}), bf16[128,16,128]{2,0,1:T(8,128)(2,1)}, u32[]{:S(2)}, u32[]{:S(2)}) %all-to-all-start.3) | async-done | bytes 524320 | tf_op jit(solution)/shard_map/all_to_all | solution.py:54
  73.4 8.0 %all-to-all-start.1 = ((bf16[128,16,128]{2,0,1:T(8,128)(2,1)}), bf16[128,16,128]{2,0,1:T(8,128)(2,1)}, u32[]{:S(2)}, u32[]{:S(2)}) async-start(bf16[128,16,128]{2,0,1:T(8,128)(2,1)} %bitcast.3), calls=%async_computation.1 | async-start | bytes 1048576 | tf_op jit(solution)/shard_map/all_to_all | solution.py:53
  82.3 12.9 %all-to-all-done.1 = bf16[128,16,128]{2,0,1:T(8,128)(2,1)} async-done(((bf16[128,16,128]{2,0,1:T(8,128)(2,1)}), bf16[128,16,128]{2,0,1:T(8,128)(2,1)}, u32[]{:S(2)}, u32[]{:S(2)}) %all-to-all-start.1) | async-done | bytes 524320 | tf_op jit(solution)/shard_map/all_to_all | solution.py:53
  95.3 8.0 %all-to-all-start.6 = ((bf16[128,16,128]{0,2,1:T(8,128)(2,1)}), bf16[128,16,128]{0,2,1:T(8,128)(2,1)S(1)}, u32[]{:S(2)}, u32[]{:S(2)}) async-start(bf16[128,16,128]{0,2,1:T(8,128)(2,1)} %bitcast.24), calls=%async_computation.6 | async-start | bytes 1048576 | tf_op jit(solution)/shard_map/all_to_all | solution.py:65
  103.3 31.5 %all_gather.3 = s32[1,2048]{1,0:T(1,128)S(1)} all-gather(s32[1,128]{1,0:T(1,128)S(1)} %copy-done.8), channel_id=1, replica_groups=mesh['dp'=16,'sp'=16] {'sp'}, dimensions={1}, use_global_device_ids=true | all-gather | bytes 8704 | tf_op jit(solution)/shard_map/all_gather | solution.py:48
  138.1 9.6 %all-to-all-start.5 = ((bf16[128,16,128]{2,0,1:T(8,128)(2,1)}), bf16[128,16,128]{2,0,1:T(8,128)(2,1)}, u32[]{:S(2)}, u32[]{:S(2)}) async-start(bf16[128,16,128]{2,0,1:T(8,128)(2,1)} %copy.87), calls=%async_computation.5 | async-start | bytes 1048576 | tf_op jit(solution)/shard_map/all_to_all | solution.py:64
  148.5 77.6 %while.34 = (s32[]{:T(128)}, f32[2048,1,128]{0,2,1:T(8,128)}, f32[2048,1,128]{0,2,1:T(8,128)}, f32[128]{0:T(128)S(1)}, bf16[4,512,1,1,128]{4,1,3,2,0:T(8,128)(2,...) while((s32[]{:T(128)}, f32[2048,1,128]{0,2,1:T(8,128)}, ...), condition=%wide.region_7.8_spmd.clone, body=%wide.region_0.7_spmd.clone.sunk | while | flops 1366883456 | bytes 68229872 | solution.py:85
  160.8 4.4 fusion.139
  172.0 2.8 fusion.136
  180.0 4.7 %fusion.139 = f32[2048,1,128]{0,2,1:T(8,128)} fusion(f32[2048,1,128]{0,2,1:T(8,128)} %get-tuple-element.728, pred[]{:T(512)S(6)} %compare.6, bf16[4,512,1,1,128]{4,1,3,2,0:T(8,128)(2,1)} %get-tuple-element.752, s32[]{:T(128)} %get-tuple-element.726, f32[1,1,512,2048]{3,2,1,0:T(8,128)} %copy-done, f32[512]{0:T(512)S(1)} %fusion.135, ...), kind=kOutput, calls=%fused_computation.17.clone.1 | convolution fusion | flops 272105472 | bytes 6427137 | tf_op jit(solution)/shard_map/while/body/eval_jaxpr/kgbs,bkgd->skd/dot_general | solution.py:24
  191.5 2.8 fusion.136
  199.5 4.7 %fusion.139 = f32[2048,1,128]{0,2,1:T(8,128)} fusion(f32[2048,1,128]{0,2,1:T(8,128)} %get-tuple-element.728, pred[]{:T(512)S(6)} %compare.6, bf16[4,512,1,1,128]{4,1,3,2,0:T(8,128)(2,1)} %get-tuple-element.752, s32[]{:T(128)} %get-tuple-element.726, f32[1,1,512,2048]{3,2,1,0:T(8,128)} %copy-done, f32[512]{0:T(512)S(1)} %fusion.135, ...), kind=kOutput, calls=%fused_computation.17.clone.1 | convolution fusion | flops 272105472 | bytes 6427137 | tf_op jit(solution)/shard_map/while/body/eval_jaxpr/kgbs,bkgd->skd/dot_general | solution.py:24
  219.0 4.7 %fusion.139 = f32[2048,1,128]{0,2,1:T(8,128)} fusion(f32[2048,1,128]{0,2,1:T(8,128)} %get-tuple-element.728, pred[]{:T(512)S(6)} %compare.6, bf16[4,512,1,1,128]{4,1,3,2,0:T(8,128)(2,1)} %get-tuple-element.752, s32[]{:T(128)} %get-tuple-element.726, f32[1,1,512,2048]{3,2,1,0:T(8,128)} %copy-done, f32[512]{0:T(512)S(1)} %fusion.135, ...), kind=kOutput, calls=%fused_computation.17.clone.1 | convolution fusion | flops 272105472 | bytes 6427137 | tf_op jit(solution)/shard_map/while/body/eval_jaxpr/kgbs,bkgd->skd/dot_general | solution.py:24
  231.8 9.6 %all-to-all-start.4 = ((bf16[16,2,8192]{2,1,0:T(2,128)(2,1)}), bf16[16,2,8192]{2,1,0:T(2,128)(2,1)}, u32[]{:S(2)}, u32[]{:S(2)}) async-start(bf16[16,2,8192]{2,1,0:T(2,128)(2,1)} %reshape.862), calls=%async_computation.4 | async-start | bytes 1048576 | tf_op jit(solution)/shard_map/all_to_all | solution.py:90
  242.3 73.3 %while.35 = (s32[]{:T(128)}, f32[2048,1,128]{0,2,1:T(8,128)S(1)}, f32[2048,1,128]{0,2,1:T(8,128)}, f32[128]{0:T(128)S(1)}, bf16[4,512,1,1,128]{4,1,3,2,0:T(8,128...) while((s32[]{:T(128)}, f32[2048,1,128]{0,2,1:T(8,128)S(1)}, ...), condition=%wide.region_15.16_spmd.clone, body=%wide.region_8.15_spmd.clone.sunk | while | flops 1366883456 | bytes 59841212 | solution.py:85
  246.6 2.8 fusion.151
  254.6 4.3 fusion.154
  272.7 4.6 fusion.154
  283.2 2.8 fusion.151
  291.1 4.6 fusion.154
  309.5 4.6 fusion.154
  318.7 9.6 %all-to-all-start.7 = ((bf16[16,2,8192]{2,1,0:T(2,128)(2,1)}), bf16[16,2,8192]{2,1,0:T(2,128)(2,1)}, u32[]{:S(2)}, u32[]{:S(2)}) async-start(bf16[16,2,8192]{2,1,0:T(2,128)(2,1)} %reshape.860), calls=%async_computation.7 | async-start | bytes 1048576 | tf_op jit(solution)/shard_map/all_to_all | solution.py:90
  332.2 10.2 %all-to-all-done.7 = bf16[16,2,8192]{2,1,0:T(2,128)(2,1)} async-done(((bf16[16,2,8192]{2,1,0:T(2,128)(2,1)}), bf16[16,2,8192]{2,1,0:T(2,128)(2,1)}, u32[]{:S(2)}, u32[]{:S(2)}) %all-to-all-start.7) | async-done | bytes 524320 | tf_op jit(solution)/shard_map/all_to_all | solution.py:90
  342.4 4.4 all-to-all-start.8
  352.1 8.6 %all-to-all-done.8 = bf16[16,2,8192]{2,1,0:T(2,128)(2,1)S(1)} async-done(((bf16[16,2,8192]{2,1,0:T(2,128)(2,1)}), bf16[16,2,8192]{2,1,0:T(2,128)(2,1)S(1)}, u32[]{:S(2)}, u32[]{:S(2)}) %all-to-all-start.8) | async-done | bytes 524320 | tf_op jit(solution)/shard_map/all_to_all | solution.py:94
  360.6 8.1 %all-to-all-start.9 = ((bf16[16,2,8192]{2,1,0:T(2,128)(2,1)}), bf16[16,2,8192]{2,1,0:T(2,128)(2,1)S(1)}, u32[]{:S(2)}, u32[]{:S(2)}) async-start(bf16[16,2,8192]{2,1,0:T(2,128)(2,1)} %reshape.866), calls=%async_computation.9 | async-start | bytes 1048576 | tf_op jit(solution)/shard_map/all_to_all | solution.py:97
  368.8 83.8 %psum.7 = f32[2,128]{1,0:T(2,128)} all-reduce(f32[2,128]{1,0:T(2,128)S(1)} %pad_maximum_fusion.1), channel_id=1, replica_groups=mesh['dp'=16,'sp'=16] {'dp','sp'}, use_global_device_ids=true, to_apply=%region_18.19 | all-reduce | flops 256 | bytes 2048 | tf_op jit(solution)/shard_map/psum | solution.py:113
  (201 shorter events, 143.2 us)
Async XLA Ops:
  1.9 33.7 %copy-start.5 = (bf16[1,128,1024]{2,1,0:T(8,128)(2,1)S(1)}, bf16[1,128,1024]{2,1,0:T(8,128)(2,1)}, u32[]{:S(2)}) copy-start(bf16[1,128,1024]{2,1,0:T(8,128)(2,1)} %param.13) | copy-start | bytes 786436
  2.9 27.6 %all-to-all-start.2 = ((bf16[128,16,128]{0,2,1:T(8,128)(2,1)}), bf16[128,16,128]{0,2,1:T(8,128)(2,1)S(1)}, u32[]{:S(2)}, u32[]{:S(2)}) async-start(bf16[128,16,128]{0,2,1:T(8,128)(2,1)} %bitcast.7), calls=%async_computation.2 | async-start | bytes 1048576 | tf_op jit(solution)/shard_map/all_to_all | solution.py:65
  15.5 43.0 %copy-start.6 = (bf16[1,128,1024]{2,1,0:T(8,128)(2,1)S(1)}, bf16[1,128,1024]{2,1,0:T(8,128)(2,1)}, u32[]{:S(2)}) copy-start(bf16[1,128,1024]{2,1,0:T(8,128)(2,1)} %param.12) | copy-start | bytes 786436
  30.6 19.0 %all-to-all-start = ((bf16[128,16,128]{2,0,1:T(8,128)(2,1)}), bf16[128,16,128]{2,0,1:T(8,128)(2,1)}, u32[]{:S(2)}, u32[]{:S(2)}) async-start(bf16[128,16,128]{2,0,1:T(8,128)(2,1)} %copy.79), calls=%async_computation | async-start | bytes 1048576 | tf_op jit(solution)/shard_map/all_to_all | solution.py:64
  35.6 67.7 %copy-start.8 = (s32[1,128]{1,0:T(1,128)S(1)}, s32[1,128]{1,0:T(1,128)}, u32[]{:S(2)}) copy-start(s32[1,128]{1,0:T(1,128)} %param.15) | copy-start | bytes 1540
  50.5 86.6 %copy-start.7 = (f32[2,128]{1,0:T(2,128)S(1)}, f32[2,128]{1,0:T(2,128)}, u32[]{:S(2)}) copy-start(f32[2,128]{1,0:T(2,128)} %param.14) | copy-start | bytes 3076
  50.5 22.0 %all-to-all-start.3 = ((bf16[128,16,128]{2,0,1:T(8,128)(2,1)}), bf16[128,16,128]{2,0,1:T(8,128)(2,1)}, u32[]{:S(2)}, u32[]{:S(2)}) async-start(bf16[128,16,128]{2,0,1:T(8,128)(2,1)} %bitcast.12), calls=%async_computation.3 | async-start | bytes 1048576 | tf_op jit(solution)/shard_map/all_to_all | solution.py:54
  73.4 21.9 %all-to-all-start.1 = ((bf16[128,16,128]{2,0,1:T(8,128)(2,1)}), bf16[128,16,128]{2,0,1:T(8,128)(2,1)}, u32[]{:S(2)}, u32[]{:S(2)}) async-start(bf16[128,16,128]{2,0,1:T(8,128)(2,1)} %bitcast.3), calls=%async_computation.1 | async-start | bytes 1048576 | tf_op jit(solution)/shard_map/all_to_all | solution.py:53
  95.3 42.9 %all-to-all-start.6 = ((bf16[128,16,128]{0,2,1:T(8,128)(2,1)}), bf16[128,16,128]{0,2,1:T(8,128)(2,1)S(1)}, u32[]{:S(2)}, u32[]{:S(2)}) async-start(bf16[128,16,128]{0,2,1:T(8,128)(2,1)} %bitcast.24), calls=%async_computation.6 | async-start | bytes 1048576 | tf_op jit(solution)/shard_map/all_to_all | solution.py:65
  138.1 10.4 %copy-start.4 = (bf16[128,16,128]{0,2,1:T(8,128)(2,1)}, bf16[128,16,128]{0,2,1:T(8,128)(2,1)S(1)}, u32[]{:S(2)}) copy-start(bf16[128,16,128]{0,2,1:T(8,128)(2,1)S(1)} %all-to-all-done.6) | copy-start | bytes 1572868
  138.1 93.7 %all-to-all-start.5 = ((bf16[128,16,128]{2,0,1:T(8,128)(2,1)}), bf16[128,16,128]{2,0,1:T(8,128)(2,1)}, u32[]{:S(2)}, u32[]{:S(2)}) async-start(bf16[128,16,128]{2,0,1:T(8,128)(2,1)} %copy.87), calls=%async_computation.5 | async-start | bytes 1048576 | tf_op jit(solution)/shard_map/all_to_all | solution.py:64
  152.1 3.5 copy-start
  160.8 4.4 copy-start.2
  166.7 1.0 copy-start.3
  171.3 3.6 copy-start
  180.0 4.7 %copy-start.2 = (f32[2048,1,128]{0,2,1:T(8,128)S(1)}, f32[2048,1,128]{0,2,1:T(8,128)}, u32[]{:S(2)}) copy-start(f32[2048,1,128]{0,2,1:T(8,128)} %get-tuple-element.727) | copy-start | bytes 3145732 | tf_op jit(solution)/shard_map/while
  186.2 1.0 copy-start.3
  190.8 3.6 copy-start
  199.5 4.7 %copy-start.2 = (f32[2048,1,128]{0,2,1:T(8,128)S(1)}, f32[2048,1,128]{0,2,1:T(8,128)}, u32[]{:S(2)}) copy-start(f32[2048,1,128]{0,2,1:T(8,128)} %get-tuple-element.727) | copy-start | bytes 3145732 | tf_op jit(solution)/shard_map/while
  205.7 1.0 copy-start.3
  210.3 3.5 copy-start
  219.0 4.7 %copy-start.2 = (f32[2048,1,128]{0,2,1:T(8,128)S(1)}, f32[2048,1,128]{0,2,1:T(8,128)}, u32[]{:S(2)}) copy-start(f32[2048,1,128]{0,2,1:T(8,128)} %get-tuple-element.727) | copy-start | bytes 3145732 | tf_op jit(solution)/shard_map/while
  225.2 1.0 copy-start.3
  231.8 86.9 %all-to-all-start.4 = ((bf16[16,2,8192]{2,1,0:T(2,128)(2,1)}), bf16[16,2,8192]{2,1,0:T(2,128)(2,1)}, u32[]{:S(2)}, u32[]{:S(2)}) async-start(bf16[16,2,8192]{2,1,0:T(2,128)(2,1)} %reshape.862), calls=%async_computation.4 | async-start | bytes 1048576 | tf_op jit(solution)/shard_map/all_to_all | solution.py:90
  245.9 3.6 copy-start.1
  264.1 3.5 copy-start.1
  282.5 3.6 copy-start.1
  300.9 3.5 copy-start.1
  318.7 23.7 %all-to-all-start.7 = ((bf16[16,2,8192]{2,1,0:T(2,128)(2,1)}), bf16[16,2,8192]{2,1,0:T(2,128)(2,1)}, u32[]{:S(2)}, u32[]{:S(2)}) async-start(bf16[16,2,8192]{2,1,0:T(2,128)(2,1)} %reshape.860), calls=%async_computation.7 | async-start | bytes 1048576 | tf_op jit(solution)/shard_map/all_to_all | solution.py:90
  342.4 18.2 %all-to-all-start.8 = ((bf16[16,2,8192]{2,1,0:T(2,128)(2,1)}), bf16[16,2,8192]{2,1,0:T(2,128)(2,1)S(1)}, u32[]{:S(2)}, u32[]{:S(2)}) async-start(bf16[16,2,8192]{2,1,0:T(2,128)(2,1)} %reshape.864), calls=%async_computation.8 | async-start | bytes 1048576 | tf_op jit(solution)/shard_map/all_to_all | solution.py:94
  360.6 100.3 %all-to-all-start.9 = ((bf16[16,2,8192]{2,1,0:T(2,128)(2,1)}), bf16[16,2,8192]{2,1,0:T(2,128)(2,1)S(1)}, u32[]{:S(2)}, u32[]{:S(2)}) async-start(bf16[16,2,8192]{2,1,0:T(2,128)(2,1)} %reshape.866), calls=%async_computation.9 | async-start | bytes 1048576 | tf_op jit(solution)/shard_map/all_to_all | solution.py:97
where the time goes:
time: 465 us; the launch traced here: 463 us
  blocking collectives  115 us (25%)
  matrix products  106 us (23%)
  starting transfers between devices  83 us (18%)
  waiting for transfers between devices  72.1 us (16%)
  other arithmetic  47.6 us (10%)
  local copies, waits for them, and re-layouts  37 us (8%)
    psum x1, blocking collectives, on_device(): dgain = lax.psum(jnp.stack(gain_list), ('dp', 'sp'))  83.8 us
    dot_general x8, matrix products, block_grads(): jnp.einsum('kgbs,bkgd->skd', prob16, dout_blk, preferred_element_type=jnp...  36.3 us
    all_gather x1, blocking collectives, on_device(): seg_all = lax.all_gather(segments, 'sp', axis=1, tiled=True)[0]  31.5 us
    dot_general x8, matrix products, block_grads(): jnp.einsum('bkgd,skd->kgbs', dout_blk, value_h, preferred_element_type=jn...  22.7 us
    all_to_all x2, starting transfers between devices, on_device(): lax.all_to_all(dout_heads[layer], 'sp', split_axis=1, concat_axis=0, tile...  20.6 us
    dot_general x8, matrix products, block_grads(): jnp.einsum('bkgd,skd->kgbs', normed, key_h, preferred_element_type=jnp.fl...  20.1 us
    all_to_all x2, starting transfers between devices, on_device(): lax.all_to_all(dq_l, 'sp', split_axis=0, concat_axis=1, tiled=True)  19.2 us
    unnamed x32, local copies, waits for them, and re-layouts  16.2 us
  transfers between devices with their start and end apart: 10, of which 6 were waited for; matrix products, arithmetic and copies ran while one was open for 39% of the time, Pallas kernels for 0%

commit v1 on v0

v1 whole, which is shorter than its diff:
```python
import functools
import math

import jax
import jax.numpy as jnp
from jax import lax
from jax.experimental import pallas as pl
from jax.experimental.pallas import tpu as pltpu
from jax.sharding import PartitionSpec as P

F32 = jnp.float32
BF16 = jnp.bfloat16
HD = 128
IDS = 16
NT = (((1,), (1,)), ((), ()))
NN = (((1,), (0,)), ((), ()))


def params(mib):
    return pltpu.CompilerParams(vmem_limit_bytes=mib << 20)


def whole():
    return pl.BlockSpec(memory_space=pltpu.VMEM)


def pack_kv_kernel(key_ref, value_ref, seg_ref, out_ref):
    parts, _, width = out_ref.shape
    rows = key_ref.shape[0]
    ids = jnp.broadcast_to(seg_ref[...].astype(F32), (IDS, rows)).astype(BF16)
    for h in range(parts):
        cols = slice(h * width, (h + 1) * width)
        out_ref[h, :rows, :] = key_ref[:, cols]
        out_ref[h, rows : 2 * rows, :] = value_ref[:, cols]
        out_ref[h, 2 * rows :, :] = ids


def pack_q_kernel(query_ref, dout_ref, out_ref):
    parts, twice, _, width = out_ref.shape
    layers = twice // 2
    for h in range(parts):
        cols = slice(h * width, (h + 1) * width)
        for layer in range(layers):
            out_ref[h, layer] = query_ref[layer, :, cols]
            out_ref[h, layers + layer] = dout_ref[layer, :, cols]


def unpack_q_kernel(in_ref, out_ref):
    parts, layers, _, width = in_ref.shape
    for h in range(parts):
        for layer in range(layers):
            out_ref[layer, :, h * width : (h + 1) * width] = in_ref[h, layer]


def combine_kernel(own_ref, cross_ref, out_ref):
    out_ref[...] = (own_ref[...] + cross_ref[...].astype(F32)).astype(BF16)


def unpack_kv_kernel(in_ref, dk_ref, dv_ref):
    parts, twice, width = in_ref.shape
    rows = twice // 2
    for h in range(parts):
        cols = slice(h * width, (h + 1) * width)
        dk_ref[:, cols] = in_ref[h, :rows, :]
        dv_ref[:, cols] = in_ref[h, rows:, :]


def attention_kernel(
    upper_ref,
    own_kv_ref,
    low_kv_ref,
    qd_ref,
    gain_ref,
    dq_ref,
    own_ref,
    cross_ref,
    dgain_ref,
    k_all,
    v_all,
    kt_all,
    start_all,
    normed,
    dout,
    score,
    dprob,
    acc,
    dqt,
):
    blocks, layers, rows, width = dq_ref.shape
    group = width // HD
    size = 2 * rows
    half = blocks // 2
    stack = layers * group * size
    scale = 1.0 / math.sqrt(HD)
    upper = upper_ref[0] > 0

    for side, ref in enumerate((low_kv_ref, own_kv_ref)):
        for b in range(half):
            at = side * half + b
            for j in range(2):
                part = slice(j * rows, (j + 1) * rows)
                kt = ref[2 * b + j, :rows, :]
                k_all[at, part, :] = kt
                v_all[at, part, :] = ref[2 * b + j, rows : 2 * rows, :]
                kt_all[at, :, part] = kt.astype(F32).T.astype(BF16)

    ids_own = jnp.concatenate(
        [own_kv_ref[b, 2 * rows :, :][:1].astype(F32) for b in range(blocks)], 0
    )
    ids_low = jnp.concatenate(
        [low_kv_ref[b, 2 * rows :, :][:1].astype(F32) for b in range(blocks)], 0
    )
    begin = jnp.zeros((blocks, rows), F32)
    for doc in range(8):
        below = jnp.sum((ids_own < doc).astype(F32), keepdims=True)
        below_low = jnp.sum((ids_low < doc).astype(F32), keepdims=True)
        total = below + jnp.where(upper, below_low, float(blocks * rows))
        begin = jnp.where(ids_own == doc, total, begin)
    for b in range(half):
        start_all[b] = jnp.concatenate([begin[2 * b : 2 * b + 1], begin[2 * b + 1 : 2 * b + 2]], 1)

    acc[...] = jnp.zeros_like(acc)
    dgain_ref[...] = jnp.zeros_like(dgain_ref)

    def part_of(i, layer, h, offset):
        cols = slice(h * HD, (h + 1) * HD)
        return jnp.concatenate(
            [qd_ref[2 * i + j, offset + layer, :, cols] for j in range(2)], 0
        )

    def norm_of(i, layer, h):
        q = part_of(i, layer, h, 0).astype(F32)
        inv = lax.rsqrt(jnp.mean(q * q, axis=-1, keepdims=True) + 1e-6)
        return q * inv, inv

    def q_block(i, carry):
        for h in range(group):
            for layer in range(layers):
                at = slice((h * layers + layer) * size, (h * layers + layer + 1) * size)
                qhat, _ = norm_of(i, layer, h)
                normed[at, :] = (qhat * gain_ref[layer : layer + 1, :]).astype(BF16)
                dout[at, :] = part_of(i, layer, h, layers)
        begin_row = start_all[i]
        first = jnp.min(begin_row).astype(jnp.int32) // size
        last = half + i
        count = last - first + 1
        begin_all = jnp.concatenate([begin_row] * (layers * group), 1).astype(jnp.int32)
        token = last * size + lax.broadcasted_iota(jnp.int32, (1, size), 1)
        token_all = jnp.concatenate([token] * (layers * group), 1)

        def scores(j, top):
            kb = first + j
            s = lax.dot_general(k_all[kb], normed[...], NT, preferred_element_type=F32)
            u = kb * size + lax.broadcasted_iota(jnp.int32, (size, stack), 0)
            s = jnp.where((u >= begin_all) & (u <= token_all), s, -1e30)
            score[j] = s
            dprob[j] = lax.dot_general(v_all[kb], dout[...], NT, preferred_element_type=F32)
            return jnp.maximum(top, jnp.max(s, axis=0, keepdims=True))

        top = lax.fori_loop(0, count, scores, jnp.full((1, stack), -1e30, F32))

        def sums(j, carry):
            total, weighted = carry
            e = jnp.exp2((score[j] - top) * (scale * math.log2(math.e)))
            score[j] = e
            return (
                total + jnp.sum(e, axis=0, keepdims=True),
                weighted + jnp.sum(e * dprob[j], axis=0, keepdims=True),
            )

        zero = jnp.zeros((1, stack), F32)
        total, weighted = lax.fori_loop(0, count, sums, (zero, zero))
        share = 1.0 / total
        delta = weighted * share
        share_scaled = share * scale
        dqt[...] = jnp.zeros_like(dqt)

        def grads(j, carry):
            kb = first + j
            e = score[j]
            prob = (e * share).astype(BF16)
            ds = (e * share_scaled * (dprob[j] - delta)).astype(BF16)
            dqt[...] += lax.dot_general(kt_all[kb], ds, NN, preferred_element_type=F32)
            for h in range(group):
                at = slice(h * layers * size, (h + 1) * layers * size)
                acc[h, 0, kb] += lax.dot_general(
                    ds[:, at], normed[at, :], NN, preferred_element_type=F32
                )
                acc[h, 1, kb] += lax.dot_general(
                    prob[:, at], dout[at, :], NN, preferred_element_type=F32
                )
            return carry

        lax.fori_loop(0, count, grads, 0)

        for h in range(group):
            for layer in range(layers):
                at = slice((h * layers + layer) * size, (h * layers + layer + 1) * size)
                dnorm = dqt[:, at].T
                qhat, inv = norm_of(i, layer, h)
                dgain_ref[layer : layer + 1, :] += jnp.sum(dnorm * qhat, axis=0, keepdims=True)
                g = dnorm * gain_ref[layer : layer + 1, :]
                dq = inv * (g - qhat * jnp.mean(g * qhat, axis=-1, keepdims=True))
                dq = dq.astype(BF16)
                cols = slice(h * HD, (h + 1) * HD)
                for j in range(2):
                    dq_ref[2 * i + j, layer, :, cols] = dq[j * rows : (j + 1) * rows]
        return carry

    lax.fori_loop(0, half, q_block, 0)

    for b in range(half):
        for j in range(2):
            part = slice(j * rows, (j + 1) * rows)
            for kv in range(2):
                out = slice(kv * rows, (kv + 1) * rows)
                whole_sum = acc[0, kv, b, part, :]
                own = acc[0, kv, half + b, part, :]
                rounded = own.astype(BF16).astype(F32)
                for h in range(1, group):
                    whole_sum = whole_sum + acc[h, kv, b, part, :]
                    own = own + acc[h, kv, half + b, part, :]
                    rounded = rounded + acc[h, kv, half + b, part, :].astype(BF16).astype(F32)
                cross_ref[2 * b + j, out, :] = whole_sum.astype(BF16)
                own_ref[2 * b + j, out, :] = jnp.where(upper, rounded, own)


def total_over_devices(x):
    cores, ys = 2, 4
    half = cores * ys
    n_sp, n_dp = lax.axis_size("sp"), lax.axis_size("dp")
    xs = 4

    def pair(x, axis, perm):
        return x + lax.ppermute(x, axis, perm)

    def ring4(x, axis, shift):
        one, two, three = (lax.ppermute(x, axis, shift(k)) for k in (1, 2, 3))
        return (x + two) + (one + three)

    x = pair(x, "sp", [(s, s ^ 1) for s in range(n_sp)])
    x = ring4(
        x,
        "sp",
        lambda k: [
            (s, s // half * half + (s % half + k * cores) % half) for s in range(n_sp)
        ],
    )
    x = ring4(x, "dp", lambda k: [(d, d // xs * xs + (d + k) % xs) for d in range(n_dp)])
    x = ring4(x, "dp", lambda k: [(d, (d + k * xs) % n_dp) for d in range(n_dp)])
    return pair(x, "sp", [(s, (s + half) % n_sp) for s in range(n_sp)])


def on_device(queries, dout, keys, values, gain, segments):
    layers, _, rows, channels = queries.shape
    n_sp = lax.axis_size("sp")
    parts = n_sp // 2
    groups = [list(range(parts)), list(range(parts, n_sp))]
    low_to_up = [(s, s + parts) for s in range(parts)]
    up_to_low = [(s + parts, s) for s in range(parts)]
    width = channels // parts
    kv_width = keys.shape[2] // parts
    half = parts // 2
    size = 2 * rows
    stack = layers * (width // HD) * size
    upper = (lax.axis_index("sp") >= parts).astype(jnp.int32).reshape(1)

    def exchange(x):
        return lax.all_to_all(x, "sp", 0, 0, axis_index_groups=groups, tiled=True)

    kv_send = pl.pallas_call(
        pack_kv_kernel,
        out_shape=jax.ShapeDtypeStruct((parts, 2 * rows + IDS, kv_width), BF16),
        in_specs=[whole()] * 3,
        out_specs=whole(),
        compiler_params=params(16),
        name="pack_kv",
    )(keys[0], values[0], segments)
    kv_own = exchange(kv_send)
    qd_send = pl.pallas_call(
        pack_q_kernel,
        out_shape=jax.ShapeDtypeStruct((parts, 2 * layers, rows, width), BF16),
        in_specs=[whole()] * 2,
        out_specs=whole(),
        compiler_params=params(16),
        name="pack_q",
    )(queries[:, 0], dout[:, 0])
    qd = exchange(qd_send)
    kv_low = lax.ppermute(kv_own, "sp", low_to_up)

    dq_send, kv_sum, cross, dgain = pl.pallas_call(
        attention_kernel,
        out_shape=(
            jax.ShapeDtypeStruct((parts, layers, rows, width), BF16),
            jax.ShapeDtypeStruct((parts, 2 * rows, kv_width), F32),
            jax.ShapeDtypeStruct((parts, 2 * rows, kv_width), BF16),
            jax.ShapeDtypeStruct((8, HD), F32),
        ),
        in_specs=[pl.BlockSpec(memory_space=pltpu.SMEM)] + [whole()] * 4,
        out_specs=(whole(),) * 4,
        scratch_shapes=[
            pltpu.VMEM((2 * half, size, HD), BF16),
            pltpu.VMEM((2 * half, size, HD), BF16),
            pltpu.VMEM((2 * half, HD, size), BF16),
            pltpu.VMEM((half, 1, size), F32),
            pltpu.VMEM((stack, HD), BF16),
            pltpu.VMEM((stack, HD), BF16),
            pltpu.VMEM((half + 1, size, stack), F32),
            pltpu.VMEM((half + 1, size, stack), F32),
            pltpu.VMEM((width // HD, 2, 2 * half, size, HD), F32),
            pltpu.VMEM((HD, stack), F32),
        ],
        compiler_params=params(48),
        name="attention",
    )(upper, kv_own, kv_low, qd, gain)

    cross_low = lax.ppermute(cross, "sp", up_to_low)
    dq_recv = exchange(dq_send)
    kv_out = pl.pallas_call(
        combine_kernel,
        out_shape=jax.ShapeDtypeStruct((parts, 2 * rows, kv_width), BF16),
        in_specs=[whole()] * 2,
        out_specs=whole(),
        compiler_params=params(16),
        name="combine",
    )(kv_sum, cross_low)
    dkv_recv = exchange(kv_out)
    dgain = total_over_devices(dgain)[:layers]
    dqueries = pl.pallas_call(
        unpack_q_kernel,
        out_shape=jax.ShapeDtypeStruct((layers, rows, channels), BF16),
        in_specs=[whole()],
        out_specs=whole(),
        compiler_params=params(16),
        name="unpack_q",
    )(dq_recv)
    dkeys, dvalues = pl.pallas_call(
        unpack_kv_kernel,
        out_shape=(jax.ShapeDtypeStruct((rows, keys.shape[2]), BF16),) * 2,
        in_specs=[whole()],
        out_specs=(whole(),) * 2,
        compiler_params=params(16),
        name="unpack_kv",
    )(dkv_recv)
    return dqueries[:, None], dkeys[None], dvalues[None], dgain


def solution(mesh):
    return jax.shard_map(
        on_device,
        mesh=mesh,
        in_specs=(
            P(None, "dp", "sp", None),
            P(None, "dp", "sp", None),
            P("dp", "sp", None),
            P("dp", "sp", None),
            P(),
            P("dp", "sp"),
        ),
        out_specs=(P(None, "dp", "sp", None), P("dp", "sp", None), P("dp", "sp", None), P()),
        check_vma=False,
    )
```

time: 465 us -> 136 us (0.29)
  blocking collectives: 115 us -> 0 us
  matrix products: 106 us -> 0 us
  other arithmetic: 47.6 us -> 0.02 us
  local copies, waits for them, and re-layouts: 37 us -> 7.37 us
  starting transfers between devices: 83 us -> 58.2 us
  waiting for transfers between devices: 72.1 us -> 48.7 us
  Pallas kernels: 0 us -> 19.1 us
    dot_general x40 -> x0, matrix products: 106 us -> none  [the longest x8 36.3 us: block_grads(): jnp.einsum('kgbs,bkgd->skd', prob16, dout_blk, preferred_element_type=jnp...]
    psum x1 -> x0, blocking collectives: 83.8 us -> none  [on_device(): dgain = lax.psum(jnp.stack(gain_list), ('dp', 'sp'))]
    all_to_all x10 -> x4, starting transfers between devices: 83 us -> 20.8 us  [exchange(): return lax.all_to_all(x, 'sp', 0, 0, axis_index_groups=groups, tiled=True)]
    all_to_all x10 -> x4, waiting for transfers between devices: 72.1 us -> 14.7 us  [exchange(): return lax.all_to_all(x, 'sp', 0, 0, axis_index_groups=groups, tiled=True)]
    ppermute x0 -> x13, starting transfers between devices: none -> 37.4 us  [the longest x9 26.6 us: ring4(): one, two, three = (lax.ppermute(x, axis, shift(k)) for k in (1, 2, 3))]
    ppermute x0 -> x13, waiting for transfers between devices: none -> 33.9 us  [the longest x1 11.1 us: on_device(): kv_low = lax.ppermute(kv_own, 'sp', low_to_up)]
    all_gather x1 -> x0, blocking collectives: 31.5 us -> none  [on_device(): seg_all = lax.all_gather(segments, 'sp', axis=1, tiled=True)[0]]
    pallas_call x0 -> x6, Pallas kernels: none -> 19.1 us  [the longest x1 15.1 us: on_device(): pl.pallas_call(attention_kernel, out_shape=(jax.ShapeDtypeStruct((parts,...]
  transfers between devices with their start and end apart: 10 -> 17, of which waited for: 6 -> 10; matrix products, arithmetic and copies ran while one was open for 39% -> 0% of each run, Pallas kernels for 0% -> 2%
where the time goes in v1:
time: 136 us; the launch traced here: 134 us
  starting transfers between devices  58.2 us (43%)
  waiting for transfers between devices  48.7 us (36%)
  Pallas kernels  19.1 us (14%)
  local copies, waits for them, and re-layouts  7.37 us (5%)
    ppermute x9, starting transfers between devices, ring4(): one, two, three = (lax.ppermute(x, axis, shift(k)) for k in (1, 2, 3))  26.6 us
    all_to_all x4, starting transfers between devices, exchange(): return lax.all_to_all(x, 'sp', 0, 0, axis_index_groups=groups, tiled=True)  20.8 us
    pallas_call x1, Pallas kernels, on_device(): pl.pallas_call(attention_kernel, out_shape=(jax.ShapeDtypeStruct((parts,...  15.1 us
    all_to_all x4, waiting for transfers between devices, exchange(): return lax.all_to_all(x, 'sp', 0, 0, axis_index_groups=groups, tiled=True)  14.7 us
    ppermute x1, waiting for transfers between devices, on_device(): kv_low = lax.ppermute(kv_own, 'sp', low_to_up)  11.1 us
    ppermute x9, waiting for transfers between devices, ring4(): one, two, three = (lax.ppermute(x, axis, shift(k)) for k in (1, 2, 3))  9.87 us
    ppermute x1, starting transfers between devices, on_device(): kv_low = lax.ppermute(kv_own, 'sp', low_to_up)  8.9 us
    ppermute x2, waiting for transfers between devices, pair(): return x + lax.ppermute(x, axis, perm)  6.97 us
  transfers between devices with their start and end apart: 17, of which 10 were waited for; matrix products, arithmetic and copies ran while one was open for 0% of the time, Pallas kernels for 2%

profile of v1, /device:TPU:1, one launch (start us, length us, event | category | flops | bytes accessed | tf_op | source)
XLA Modules:
  0.0 134.2 jit_solution(1663320332179761278)
XLA Ops:
  0.7 1.1 copy-done.6
  1.8 0.9 copy-done.7
  3.4 0.9 pack_kv.1
  4.3 6.7 %all-to-all-start = ((bf16[8,272,128]{2,1,0:T(8,128)(2,1)}), bf16[8,272,128]{2,1,0:T(8,128)(2,1)S(1)}, u32[]{:S(2)}, u32[]{:S(2)}) async-start(bf16[8,272,128]{2,1,0:T(8,128)(2,1)} %pack_kv.1), calls=%async_computation | async-start | bytes 1114112 | tf_op jit(solution)/shard_map/all_to_all | solution.py:269
  11.1 1.3 %copy-done = bf16[8,4,128,256]{3,2,1,0:T(8,128)(2,1)} copy-done((bf16[8,4,128,256]{3,2,1,0:T(8,128)(2,1)}, bf16[8,4,128,256]{3,2,1,0:T(8,128)(2,1)S(1)}, u32[]{:S(2)}) %copy-start) | copy-done | bytes 2097176
  12.5 8.3 %all-to-all-done.own_kv_ref = bf16[8,272,128]{2,1,0:T(8,128)(2,1)S(1)} async-done(((bf16[8,272,128]{2,1,0:T(8,128)(2,1)}), bf16[8,272,128]{2,1,0:T(8,128)(2,1)S(1)}, u32[]{:S(2)}, u32[]{:S(2)}) %all-to-all-start) | async-done | bytes 557088 | tf_op jit(solution)/shard_map/all_to_all | solution.py:269
  20.8 4.4 %all-to-all-start.1 = ((bf16[8,4,128,256]{3,2,1,0:T(8,128)(2,1)}), bf16[8,4,128,256]{3,2,1,0:T(8,128)(2,1)S(1)}, u32[]{:S(2)}, u32[]{:S(2)}) async-start(bf16[8,4,128,256]{3,2,1,0:T(8,128)(2,1)} %copy-done), calls=%async_computation.1 | async-start | bytes 4194304 | tf_op jit(solution)/shard_map/all_to_all | solution.py:269
  25.2 8.9 %collective-permute-start = (bf16[8,272,128]{2,1,0:T(8,128)(2,1)S(1)}, bf16[8,272,128]{2,1,0:T(8,128)(2,1)}, u32[]{:S(2)}, u32[]{:S(2)}) collective-permute-start(bf16[8,272,128]{2,1,0:T(8,128)(2,1)S(1)} %all-to-all-done.own_kv_ref), channel_id=1, source_target_pairs={{0,8},{1,9},{2,10},{3,11},{4,12},{5,13},{6,14},{7,15},{16,24},{17,... | collective-permute-start | bytes 1671176 | tf_op jit(solution)/shard_map/ppermute | solution.py:289
  34.1 11.1 %collective-permute-done.low_kv_ref = bf16[8,272,128]{2,1,0:T(8,128)(2,1)} collective-permute-done((bf16[8,272,128]{2,1,0:T(8,128)(2,1)S(1)}, bf16[8,272,128]{2,1,0:T(8,128)(2,1)}, u32[]{:S(2)}, u32[]{:S(2)}) %collective-permute-start) | collective-permute-done | bytes 557088 | tf_op jit(solution)/shard_map/ppermute | solution.py:289
  45.1 6.4 %all-to-all-done.1.qd_ref = bf16[8,4,128,256]{3,2,1,0:T(8,128)(2,1)S(1)} async-done(((bf16[8,4,128,256]{3,2,1,0:T(8,128)(2,1)}), bf16[8,4,128,256]{3,2,1,0:T(8,128)(2,1)S(1)}, u32[]{:S(2)}, u32[]{:S(2)}) %all-to-all-start.1) | async-done | bytes 2097184 | tf_op jit(solution)/shard_map/all_to_all | solution.py:269
  51.5 15.1 %attention.1 = (bf16[8,2,128,256]{3,2,1,0:T(8,128)(2,1)S(1)}, f32[8,256,128]{2,1,0:T(8,128)S(1)}, bf16[8,256,128]{2,1,0:T(8,128)(2,1)S(1)}, f32[8,128]{1,0:T(8,128)S(1)}) custom-call(s32[1]{0:T(128)} %bitcast.upper_ref, bf16[8,272,128]{2,1,0:T(8,128)(2,1)S(1)} %all-to-all-done.own_kv_ref, bf16[8,272,128]{2,1,0:T(8,128)(2,1)} %collective-permute-done.low_kv_ref, ...), custom_call_target="tpu_custom_call" | custom-call | tf_op jit(solution)/shard_map/attention/pallas_call | solution.py:291
  66.7 1.0 copy-done.1
  67.6 1.0 copy-done.2
  68.6 0.8 copy-done.10
  69.4 4.5 %all-to-all-start.2 = ((bf16[8,2,128,256]{3,2,1,0:T(8,128)(2,1)}), bf16[8,2,128,256]{3,2,1,0:T(8,128)(2,1)S(1)}, u32[]{:S(2)}, u32[]{:S(2)}) async-start(bf16[8,2,128,256]{3,2,1,0:T(8,128)(2,1)} %copy-done.1), calls=%async_computation.2 | async-start | bytes 2097152 | tf_op jit(solution)/shard_map/all_to_all | solution.py:269
  73.9 1.3 collective-permute-start.1
  75.4 1.0 collective-permute-done.2
  76.5 2.6 %collective-permute-start.5 = (f32[8,128]{1,0:T(8,128)S(1)}, f32[8,128]{1,0:T(8,128)S(1)}, u32[]{:S(2)}, u32[]{:S(2)}) collective-permute-start(f32[8,128]{1,0:T(8,128)S(1)} %add.33), channel_id=1, source_target_pairs={{0,6},{1,7},{2,0},{3,1},{4,2},{5,3},{6,4},{7,5},{8,14},{9,15},{10,... | collective-permute-start | bytes 12296 | tf_op jit(solution)/shard_map/ppermute | solution.py:238
  79.1 1.7 %collective-permute-start.3 = (f32[8,128]{1,0:T(8,128)S(1)}, f32[8,128]{1,0:T(8,128)S(1)}, u32[]{:S(2)}, u32[]{:S(2)}) collective-permute-start(f32[8,128]{1,0:T(8,128)S(1)} %add.33), channel_id=1, source_target_pairs={{0,4},{1,5},{2,6},{3,7},{4,0},{5,1},{6,2},{7,3},{8,12},{9,13},{10,... | collective-permute-start | bytes 12296 | tf_op jit(solution)/shard_map/ppermute | solution.py:238
  80.8 6.7 %collective-permute-done.5 = f32[8,128]{1,0:T(8,128)S(1)} collective-permute-done((f32[8,128]{1,0:T(8,128)S(1)}, f32[8,128]{1,0:T(8,128)S(1)}, u32[]{:S(2)}, u32[]{:S(2)}) %collective-permute-start.5) | collective-permute-done | bytes 4128 | tf_op jit(solution)/shard_map/ppermute | solution.py:238
  87.6 1.6 %collective-permute-done.3 = f32[8,128]{1,0:T(8,128)S(1)} collective-permute-done((f32[8,128]{1,0:T(8,128)S(1)}, f32[8,128]{1,0:T(8,128)S(1)}, u32[]{:S(2)}, u32[]{:S(2)}) %collective-permute-start.3) | collective-permute-done | bytes 4128 | tf_op jit(solution)/shard_map/ppermute | solution.py:238
  89.2 1.7 %collective-permute-start.8 = (f32[8,128]{1,0:T(8,128)S(1)}, f32[8,128]{1,0:T(8,128)S(1)}, u32[]{:S(2)}, u32[]{:S(2)}) collective-permute-start(f32[8,128]{1,0:T(8,128)S(1)} %add_add_fusion.2), channel_id=1, source_target_pairs={{0,48},{16,0},{32,16},{48,32},{64,112},{80,64},{96,80},{112,96},{1... | collective-permute-start | bytes 12296 | tf_op jit(solution)/shard_map/ppermute | solution.py:238
  91.1 5.5 %collective-permute-start.6 = (f32[8,128]{1,0:T(8,128)S(1)}, f32[8,128]{1,0:T(8,128)S(1)}, u32[]{:S(2)}, u32[]{:S(2)}) collective-permute-start(f32[8,128]{1,0:T(8,128)S(1)} %add_add_fusion.2), channel_id=1, source_target_pairs={{0,32},{16,48},{32,0},{48,16},{64,96},{80,112},{96,64},{112,80},{1... | collective-permute-start | bytes 12296 | tf_op jit(solution)/shard_map/ppermute | solution.py:238
  96.6 6.0 %collective-permute-done.1.cross_ref = bf16[8,256,128]{2,1,0:T(8,128)(2,1)S(1)} collective-permute-done((bf16[8,256,128]{2,1,0:T(8,128)(2,1)S(1)}, bf16[8,256,128]{2,1,0:T(8,128)(2,1)S(1)}, u32[]{:S(2)}, u32[]{:S(2)}) %collective-permute-start.1) | collective-permute-done | bytes 524320 | tf_op jit(solution)/shard_map/ppermute | solution.py:317
  102.6 0.9 combine.1
  103.5 5.3 %all-to-all-start.3 = ((bf16[8,256,128]{2,1,0:T(8,128)(2,1)}), bf16[8,256,128]{2,1,0:T(8,128)(2,1)S(1)}, u32[]{:S(2)}, u32[]{:S(2)}) async-start(bf16[8,256,128]{2,1,0:T(8,128)(2,1)} %combine.1), calls=%async_computation.3 | async-start | bytes 1048576 | tf_op jit(solution)/shard_map/all_to_all | solution.py:269
  108.8 1.7 %collective-permute-start.11 = (f32[8,128]{1,0:T(8,128)S(1)}, f32[8,128]{1,0:T(8,128)S(1)}, u32[]{:S(2)}, u32[]{:S(2)}) collective-permute-start(f32[8,128]{1,0:T(8,128)S(1)} %add_add_fusion.1), channel_id=1, source_target_pairs={{0,192},{16,208},{32,224},{48,240},{64,0},{80,16},{96,32},{112,48}... | collective-permute-start | bytes 12296 | tf_op jit(solution)/shard_map/ppermute | solution.py:238
  110.5 11.2 %collective-permute-start.10 = (f32[8,128]{1,0:T(8,128)S(1)}, f32[8,128]{1,0:T(8,128)S(1)}, u32[]{:S(2)}, u32[]{:S(2)}) collective-permute-start(f32[8,128]{1,0:T(8,128)S(1)} %add_add_fusion.1), channel_id=1, source_target_pairs={{0,64},{16,80},{32,96},{48,112},{64,128},{80,144},{96,160},{112,17... | collective-permute-start | bytes 12296 | tf_op jit(solution)/shard_map/ppermute | solution.py:238
  121.8 1.9 %collective-permute-start.9 = (f32[8,128]{1,0:T(8,128)S(1)}, f32[8,128]{1,0:T(8,128)S(1)}, u32[]{:S(2)}, u32[]{:S(2)}) collective-permute-start(f32[8,128]{1,0:T(8,128)S(1)} %add_add_fusion.1), channel_id=1, source_target_pairs={{0,128},{16,144},{32,160},{48,176},{64,192},{80,208},{96,224},{112... | collective-permute-start | bytes 12296 | tf_op jit(solution)/shard_map/ppermute | solution.py:238
  125.6 5.9 %collective-permute-done.12 = f32[8,128]{1,0:T(8,128)S(1)} collective-permute-done((f32[8,128]{1,0:T(8,128)S(1)}, f32[8,128]{1,0:T(8,128)S(1)}, u32[]{:S(2)}, u32[]{:S(2)}) %collective-permute-start.12) | collective-permute-done | bytes 4128 | tf_op jit(solution)/shard_map/ppermute | solution.py:235
  132.1 1.1 unpack_q.1
  133.2 0.9 unpack_kv.1
  (38 shorter events, 3.7 us)
Async XLA Ops:
  0.6 10.3 %copy-start.5 = (bf16[2,1,128,2048]{3,2,1,0:T(8,128)(2,1)S(1)}, bf16[2,1,128,2048]{3,2,1,0:T(8,128)(2,1)}, u32[]{:S(2)}) copy-start(bf16[2,1,128,2048]{3,2,1,0:T(8,128)(2,1)} %param.7) | copy-start | bytes 3145732
  0.6 10.3 %copy-start.4 = (bf16[2,1,128,2048]{3,2,1,0:T(8,128)(2,1)S(1)}, bf16[2,1,128,2048]{3,2,1,0:T(8,128)(2,1)}, u32[]{:S(2)}) copy-start(bf16[2,1,128,2048]{3,2,1,0:T(8,128)(2,1)} %param.6) | copy-start | bytes 3145732
  0.7 1.1 copy-start.6
  1.7 0.9 copy-start.7
  2.7 0.7 copy-start.9
  4.3 16.5 %all-to-all-start = ((bf16[8,272,128]{2,1,0:T(8,128)(2,1)}), bf16[8,272,128]{2,1,0:T(8,128)(2,1)S(1)}, u32[]{:S(2)}, u32[]{:S(2)}) async-start(bf16[8,272,128]{2,1,0:T(8,128)(2,1)} %pack_kv.1), calls=%async_computation | async-start | bytes 1114112 | tf_op jit(solution)/shard_map/all_to_all | solution.py:269
  11.1 1.4 %copy-start = (bf16[8,4,128,256]{3,2,1,0:T(8,128)(2,1)}, bf16[8,4,128,256]{3,2,1,0:T(8,128)(2,1)S(1)}, u32[]{:S(2)}) copy-start(bf16[8,4,128,256]{3,2,1,0:T(8,128)(2,1)S(1)} %pack_q.1) | copy-start | bytes 6291460
  12.5 39.1 %copy-start.8 = (f32[2,128]{1,0:T(2,128)S(1)}, f32[2,128]{1,0:T(2,128)}, u32[]{:S(2)}) copy-start(f32[2,128]{1,0:T(2,128)} %gain_ref.1) | copy-start | bytes 3076
  20.8 30.7 %all-to-all-start.1 = ((bf16[8,4,128,256]{3,2,1,0:T(8,128)(2,1)}), bf16[8,4,128,256]{3,2,1,0:T(8,128)(2,1)S(1)}, u32[]{:S(2)}, u32[]{:S(2)}) async-start(bf16[8,4,128,256]{3,2,1,0:T(8,128)(2,1)} %copy-done), calls=%async_computation.1 | async-start | bytes 4194304 | tf_op jit(solution)/shard_map/all_to_all | solution.py:269
  25.2 20.0 %collective-permute-start = (bf16[8,272,128]{2,1,0:T(8,128)(2,1)S(1)}, bf16[8,272,128]{2,1,0:T(8,128)(2,1)}, u32[]{:S(2)}, u32[]{:S(2)}) collective-permute-start(bf16[8,272,128]{2,1,0:T(8,128)(2,1)S(1)} %all-to-all-done.own_kv_ref), channel_id=1, source_target_pairs={{0,8},{1,9},{2,10},{3,11},{4,12},{5,13},{6,14},{7,15},{16,24},{17,... | collective-permute-start | bytes 1671176 | tf_op jit(solution)/shard_map/ppermute | solution.py:289
  66.7 1.0 copy-start.1
  67.6 1.0 copy-start.2
  68.6 0.8 copy-start.10
  69.4 4.5 %copy-start.11 = (bf16[8,256,128]{2,1,0:T(8,128)(2,1)S(1)}, bf16[8,256,128]{2,1,0:T(8,128)(2,1)}, u32[]{:S(2)}) copy-start(bf16[8,256,128]{2,1,0:T(8,128)(2,1)} %copy-done.10) | copy-start | bytes 1572868
  69.4 33.2 %copy-start.3 = (f32[8,256,128]{2,1,0:T(8,128)S(1)}, f32[8,256,128]{2,1,0:T(8,128)}, u32[]{:S(2)}) copy-start(f32[8,256,128]{2,1,0:T(8,128)} %copy-done.2) | copy-start | bytes 3145732
  69.4 34.1 %all-to-all-start.2 = ((bf16[8,2,128,256]{3,2,1,0:T(8,128)(2,1)}), bf16[8,2,128,256]{3,2,1,0:T(8,128)(2,1)S(1)}, u32[]{:S(2)}, u32[]{:S(2)}) async-start(bf16[8,2,128,256]{3,2,1,0:T(8,128)(2,1)} %copy-done.1), calls=%async_computation.2 | async-start | bytes 2097152 | tf_op jit(solution)/shard_map/all_to_all | solution.py:269
  73.9 28.7 %collective-permute-start.1 = (bf16[8,256,128]{2,1,0:T(8,128)(2,1)S(1)}, bf16[8,256,128]{2,1,0:T(8,128)(2,1)S(1)}, u32[]{:S(2)}, u32[]{:S(2)}) collective-permute-start(bf16[8,256,128]{2,1,0:T(8,128)(2,1)S(1)} %copy-done.11), channel_id=1, source_target_pairs={{8,0},{9,1},{10,2},{11,3},{12,4},{13,5},{14,6},{15,7},{24,16},{25,... | collective-permute-start | bytes 1572872 | tf_op jit(solution)/shard_map/ppermute | solution.py:317
  75.2 1.3 collective-permute-start.2
  76.5 11.1 %collective-permute-start.5 = (f32[8,128]{1,0:T(8,128)S(1)}, f32[8,128]{1,0:T(8,128)S(1)}, u32[]{:S(2)}, u32[]{:S(2)}) collective-permute-start(f32[8,128]{1,0:T(8,128)S(1)} %add.33), channel_id=1, source_target_pairs={{0,6},{1,7},{2,0},{3,1},{4,2},{5,3},{6,4},{7,5},{8,14},{9,15},{10,... | collective-permute-start | bytes 12296 | tf_op jit(solution)/shard_map/ppermute | solution.py:238
  79.1 8.5 %collective-permute-start.4 = (f32[8,128]{1,0:T(8,128)S(1)}, f32[8,128]{1,0:T(8,128)S(1)}, u32[]{:S(2)}, u32[]{:S(2)}) collective-permute-start(f32[8,128]{1,0:T(8,128)S(1)} %add.33), channel_id=1, source_target_pairs={{0,2},{1,3},{2,4},{3,5},{4,6},{5,7},{6,0},{7,1},{8,10},{9,11},{10,... | collective-permute-start | bytes 12296 | tf_op jit(solution)/shard_map/ppermute | solution.py:238
  79.1 10.1 %collective-permute-start.3 = (f32[8,128]{1,0:T(8,128)S(1)}, f32[8,128]{1,0:T(8,128)S(1)}, u32[]{:S(2)}, u32[]{:S(2)}) collective-permute-start(f32[8,128]{1,0:T(8,128)S(1)} %add.33), channel_id=1, source_target_pairs={{0,4},{1,5},{2,6},{3,7},{4,0},{5,1},{6,2},{7,3},{8,12},{9,13},{10,... | collective-permute-start | bytes 12296 | tf_op jit(solution)/shard_map/ppermute | solution.py:238
  89.2 19.6 %collective-permute-start.8 = (f32[8,128]{1,0:T(8,128)S(1)}, f32[8,128]{1,0:T(8,128)S(1)}, u32[]{:S(2)}, u32[]{:S(2)}) collective-permute-start(f32[8,128]{1,0:T(8,128)S(1)} %add_add_fusion.2), channel_id=1, source_target_pairs={{0,48},{16,0},{32,16},{48,32},{64,112},{80,64},{96,80},{112,96},{1... | collective-permute-start | bytes 12296 | tf_op jit(solution)/shard_map/ppermute | solution.py:238
  90.9 17.8 %collective-permute-start.7 = (f32[8,128]{1,0:T(8,128)S(1)}, f32[8,128]{1,0:T(8,128)S(1)}, u32[]{:S(2)}, u32[]{:S(2)}) collective-permute-start(f32[8,128]{1,0:T(8,128)S(1)} %add_add_fusion.2), channel_id=1, source_target_pairs={{0,16},{16,32},{32,48},{48,0},{64,80},{80,96},{96,112},{112,64},{1... | collective-permute-start | bytes 12296 | tf_op jit(solution)/shard_map/ppermute | solution.py:238
  91.1 17.7 %collective-permute-start.6 = (f32[8,128]{1,0:T(8,128)S(1)}, f32[8,128]{1,0:T(8,128)S(1)}, u32[]{:S(2)}, u32[]{:S(2)}) collective-permute-start(f32[8,128]{1,0:T(8,128)S(1)} %add_add_fusion.2), channel_id=1, source_target_pairs={{0,32},{16,48},{32,0},{48,16},{64,96},{80,112},{96,64},{112,80},{1... | collective-permute-start | bytes 12296 | tf_op jit(solution)/shard_map/ppermute | solution.py:238
  103.5 29.7 %all-to-all-start.3 = ((bf16[8,256,128]{2,1,0:T(8,128)(2,1)}), bf16[8,256,128]{2,1,0:T(8,128)(2,1)S(1)}, u32[]{:S(2)}, u32[]{:S(2)}) async-start(bf16[8,256,128]{2,1,0:T(8,128)(2,1)} %combine.1), calls=%async_computation.3 | async-start | bytes 1048576 | tf_op jit(solution)/shard_map/all_to_all | solution.py:269
  108.8 14.9 %collective-permute-start.11 = (f32[8,128]{1,0:T(8,128)S(1)}, f32[8,128]{1,0:T(8,128)S(1)}, u32[]{:S(2)}, u32[]{:S(2)}) collective-permute-start(f32[8,128]{1,0:T(8,128)S(1)} %add_add_fusion.1), channel_id=1, source_target_pairs={{0,192},{16,208},{32,224},{48,240},{64,0},{80,16},{96,32},{112,48}... | collective-permute-start | bytes 12296 | tf_op jit(solution)/shard_map/ppermute | solution.py:238
  110.5 13.9 %collective-permute-start.10 = (f32[8,128]{1,0:T(8,128)S(1)}, f32[8,128]{1,0:T(8,128)S(1)}, u32[]{:S(2)}, u32[]{:S(2)}) collective-permute-start(f32[8,128]{1,0:T(8,128)S(1)} %add_add_fusion.1), channel_id=1, source_target_pairs={{0,64},{16,80},{32,96},{48,112},{64,128},{80,144},{96,160},{112,17... | collective-permute-start | bytes 12296 | tf_op jit(solution)/shard_map/ppermute | solution.py:238
  121.8 3.4 %collective-permute-start.9 = (f32[8,128]{1,0:T(8,128)S(1)}, f32[8,128]{1,0:T(8,128)S(1)}, u32[]{:S(2)}, u32[]{:S(2)}) collective-permute-start(f32[8,128]{1,0:T(8,128)S(1)} %add_add_fusion.1), channel_id=1, source_target_pairs={{0,128},{16,144},{32,160},{48,176},{64,192},{80,208},{96,224},{112... | collective-permute-start | bytes 12296 | tf_op jit(solution)/shard_map/ppermute | solution.py:238
  125.2 6.4 %collective-permute-start.12 = (f32[8,128]{1,0:T(8,128)S(1)}, f32[8,128]{1,0:T(8,128)S(1)}, u32[]{:S(2)}, u32[]{:S(2)}) collective-permute-start(f32[8,128]{1,0:T(8,128)S(1)} %add_add_fusion), channel_id=1, source_target_pairs={{0,8},{1,9},{2,10},{3,11},{4,12},{5,13},{6,14},{7,15},{8,0},{9,1},... | collective-permute-start | bytes 12296 | tf_op jit(solution)/shard_map/ppermute | solution.py:235

commit v2 on v1

v2 whole, which is shorter than its diff:
```python
import functools
import math

import jax
import jax.numpy as jnp
from jax import lax
from jax.experimental import pallas as pl
from jax.experimental.pallas import tpu as pltpu
from jax.sharding import PartitionSpec as P

F32 = jnp.float32
BF16 = jnp.bfloat16
HD = 128
IDS = 16
PIECES = 3
GAIN_ROWS = 8
NT = (((1,), (1,)), ((), ()))
NN = (((1,), (0,)), ((), ()))


def params(mib):
    return pltpu.CompilerParams(vmem_limit_bytes=mib << 20)


def in_hbm():
    return pl.BlockSpec(memory_space=pltpu.HBM)


def whole():
    return pl.BlockSpec(memory_space=pltpu.VMEM)


def pack_kv_kernel(key_ref, value_ref, seg_ref, out_ref):
    parts, _, width = out_ref.shape
    rows = key_ref.shape[0]
    ids = jnp.broadcast_to(seg_ref[...].astype(F32), (IDS, rows)).astype(BF16)
    for h in range(parts):
        cols = slice(h * width, (h + 1) * width)
        out_ref[h, :rows, :] = key_ref[:, cols]
        out_ref[h, rows : 2 * rows, :] = value_ref[:, cols]
        out_ref[h, 2 * rows :, :] = ids


def pack_q_kernel(query_ref, dout_ref, out_ref):
    parts, twice, _, width = out_ref.shape
    layers = twice // 2
    for h in range(parts):
        cols = slice(h * width, (h + 1) * width)
        for layer in range(layers):
            out_ref[h, layer] = query_ref[layer, :, cols]
            out_ref[h, layers + layer] = dout_ref[layer, :, cols]


def unpack_q_kernel(in_ref, out_ref):
    parts, layers, _, width = in_ref.shape
    for h in range(parts):
        for layer in range(layers):
            out_ref[layer, :, h * width : (h + 1) * width] = in_ref[h, layer]


def combine_kernel(own_ref, cross_ref, dgain_ref, out_ref):
    twice = own_ref.shape[1]
    out_ref[:, :twice, :] = (own_ref[...] + cross_ref[...].astype(F32)).astype(BF16)
    rest = dgain_ref[...]
    pieces = []
    for _ in range(PIECES):
        piece = rest.astype(BF16).astype(F32)
        rest = rest - piece
        pieces.append(piece)
    pieces = jnp.concatenate(pieces + [jnp.zeros_like(rest)], 0).astype(BF16)
    for h in range(out_ref.shape[0]):
        out_ref[h, twice:, :] = pieces


def unpack_kv_kernel(in_ref, dk_ref, dv_ref, dgain_ref):
    parts, _, width = in_ref.shape
    rows = dk_ref.shape[0]
    total = jnp.zeros((GAIN_ROWS, width), F32)
    for h in range(parts):
        cols = slice(h * width, (h + 1) * width)
        dk_ref[:, cols] = in_ref[h, :rows, :]
        dv_ref[:, cols] = in_ref[h, rows : 2 * rows, :]
        pieces = in_ref[h, 2 * rows :, :].astype(F32)
        for n in range(PIECES):
            total = total + pieces[n * GAIN_ROWS : (n + 1) * GAIN_ROWS]
    dgain_ref[...] = total[: dgain_ref.shape[0]]


def attention_kernel(
    upper_ref,
    own_kv_ref,
    low_kv_ref,
    qd_ref,
    gain_ref,
    dq_ref,
    own_ref,
    cross_ref,
    dgain_ref,
    k_all,
    v_all,
    kt_all,
    start_all,
    qhat_t,
    inv_row,
    normed_t,
    dout,
    expo,
    dprob,
    tops,
    acc,
    dq_t,
    gain_acc,
    dq_out,
    own_out,
    cross_out,
    sem,
):
    blocks, layers, rows, width = dq_ref.shape
    group = width // HD
    size = 2 * rows
    half = blocks // 2
    scale = 1.0 / math.sqrt(HD)
    rate = scale * math.log2(math.e)
    upper = upper_ref[0] > 0
    chunks = [
        (slice((h * layers + layer) * size, (h * layers + layer + 1) * size), h, layer)
        for h in range(group)
        for layer in range(layers)
    ]

    def eye(n):
        at = lax.broadcasted_iota(jnp.int32, (n, n), 0)
        return (at == lax.broadcasted_iota(jnp.int32, (n, n), 1)).astype(F32)

    def dot(a, b, dims):
        return lax.dot_general(a, b, dims, preferred_element_type=F32)

    unit = eye(HD).astype(BF16)
    unit_size = eye(size).astype(BF16)
    gain_cols = [
        jnp.sum(eye(HD) * gain_ref[layer : layer + 1, :], axis=1, keepdims=True)
        for layer in range(layers)
    ]

    for side, ref in enumerate((low_kv_ref, own_kv_ref)):
        for b in range(half):
            at = side * half + b
            for j in range(2):
                part = slice(j * rows, (j + 1) * rows)
                k_all[at, part, :] = ref[2 * b + j, :rows, :]
                v_all[at, part, :] = ref[2 * b + j, rows : 2 * rows, :]
            kt_all[at] = dot(unit, k_all[at], NT).astype(BF16)

    ids_own = jnp.concatenate(
        [own_kv_ref[b, 2 * rows :, :][:1].astype(F32) for b in range(blocks)], 0
    )
    ids_low = jnp.concatenate(
        [low_kv_ref[b, 2 * rows :, :][:1].astype(F32) for b in range(blocks)], 0
    )
    begin = jnp.zeros((blocks, rows), F32)
    for doc in range(8):
        below = jnp.sum((ids_own < doc).astype(F32), keepdims=True)
        below_low = jnp.sum((ids_low < doc).astype(F32), keepdims=True)
        total = below + jnp.where(upper, below_low, float(blocks * rows))
        begin = jnp.where(ids_own == doc, total, begin)
    for b in range(half):
        start_all[b] = jnp.concatenate([begin[2 * b : 2 * b + 1], begin[2 * b + 1 : 2 * b + 2]], 1)

    acc[...] = jnp.zeros_like(acc)
    gain_acc[...] = jnp.zeros_like(gain_acc)

    def part_of(i, layer, h, offset):
        cols = slice(h * HD, (h + 1) * HD)
        return jnp.concatenate(
            [qd_ref[2 * i + j, offset + layer, :, cols] for j in range(2)], 0
        )

    def q_block(i, carry):
        for at, h, layer in chunks:
            q = dot(unit, part_of(i, layer, h, 0), NT)
            inv = lax.rsqrt(jnp.mean(q * q, axis=0, keepdims=True) + 1e-6)
            qhat = q * inv
            inv_row[:, at] = inv
            qhat_t[:, at] = qhat
            normed_t[:, at] = (qhat * gain_cols[layer]).astype(BF16)
            dout[at, :] = part_of(i, layer, h, layers)
        begin_row = start_all[i]
        first = jnp.min(begin_row).astype(jnp.int32) // size
        last = half + i
        count = last - first + 1
        begin_int = begin_row.astype(jnp.int32)
        token = last * size + lax.broadcasted_iota(jnp.int32, (1, size), 1)
        dq_t[...] = jnp.zeros_like(dq_t)

        def sums(j, carry):
            kb = first + j
            k, v = k_all[kb], v_all[kb]
            u = kb * size + lax.broadcasted_iota(jnp.int32, (size, size), 0)
            bias = jnp.where((u >= begin_int) & (u <= token), 0.0, -1e30)
            out = []
            for (at, _, _), (top, total, weighted) in zip(chunks, carry):
                s = dot(k, normed_t[:, at], NN) + bias
                dp = dot(v, dout[at, :], NT)
                new = jnp.maximum(top, jnp.max(s, axis=0, keepdims=True))
                e = jnp.exp2((s - new) * rate)
                keep = jnp.exp2((top - new) * rate)
                expo[j, :, at] = e
                dprob[j, :, at] = dp
                tops[j, :, at] = new
                out.append(
                    (
                        new,
                        total * keep + jnp.sum(e, axis=0, keepdims=True),
                        weighted * keep + jnp.sum(e * dp, axis=0, keepdims=True),
                    )
                )
            return tuple(out)

        zero = jnp.zeros((1, size), F32)
        low = jnp.full((1, size), -1e30, F32)
        stats = lax.fori_loop(0, count, sums, ((low, zero, zero),) * len(chunks))
        shares = [1.0 / total for _, total, _ in stats]
        deltas = [weighted * share for (_, _, weighted), share in zip(stats, shares)]

        def grads(j, carry):
            kb = first + j
            kt = kt_all[kb]
            probs, scores = [], []
            for (at, _, _), (top, _, _), share, delta in zip(chunks, stats, shares, deltas):
                prob = expo[j, :, at] * (share * jnp.exp2((tops[j, :, at] - top) * rate))
                ds = (prob * ((dprob[j, :, at] - delta) * scale)).astype(BF16)
                probs.append(prob.astype(BF16))
                scores.append(ds)
                dq_t[:, at] += dot(kt, ds, NN)
            for h in range(group):
                at = slice(h * layers * size, (h + 1) * layers * size)
                mine = slice(h * layers, (h + 1) * layers)
                ds = jnp.concatenate(scores[mine], 1)
                prob = jnp.concatenate(probs[mine], 1)
                acc[h, 0, kb] += dot(ds, normed_t[:, at], NT)
                acc[h, 1, kb] += dot(prob, dout[at, :], NN)
            return carry

        lax.fori_loop(0, count, grads, 0)

        for at, h, layer in chunks:
            dnorm, qhat = dq_t[:, at], qhat_t[:, at]
            part = dnorm * qhat
            gain_acc[layer] += part[:, :rows] + part[:, rows:]
            g = dnorm * gain_cols[layer]
            dq = inv_row[:, at] * (g - qhat * jnp.mean(g * qhat, axis=0, keepdims=True))
            dq = dot(unit_size, dq.astype(BF16), NT).astype(BF16)
            cols = slice(h * HD, (h + 1) * HD)
            for j in range(2):
                dq_out[2 * i + j, layer, :, cols] = dq[j * rows : (j + 1) * rows]
        pair = pl.ds(2 * i, 2)
        pltpu.make_async_copy(dq_out.at[pair], dq_ref.at[pair], sem.at[i]).start()
        return carry

    lax.fori_loop(0, half, q_block, 0)

    dgain_ref[...] = jnp.zeros_like(dgain_ref)
    for layer in range(layers):
        dgain_ref[layer : layer + 1, :] = jnp.sum(gain_acc[layer].T, axis=0, keepdims=True)
    copies = []
    for b in range(half):
        for j in range(2):
            part = slice(j * rows, (j + 1) * rows)
            for kv in range(2):
                out = slice(kv * rows, (kv + 1) * rows)
                whole_sum = acc[0, kv, b, part, :]
                own = acc[0, kv, half + b, part, :]
                rounded = own.astype(BF16).astype(F32)
                for h in range(1, group):
                    whole_sum = whole_sum + acc[h, kv, b, part, :]
                    own = own + acc[h, kv, half + b, part, :]
                    rounded = rounded + acc[h, kv, half + b, part, :].astype(BF16).astype(F32)
                cross_out[2 * b + j, out, :] = whole_sum.astype(BF16)
                own_out[2 * b + j, out, :] = jnp.where(upper, rounded, own)
        pair = pl.ds(2 * b, 2)
        for n, (src, dst) in enumerate(((cross_out, cross_ref), (own_out, own_ref))):
            copy = pltpu.make_async_copy(src.at[pair], dst.at[pair], sem.at[half * (n + 1) + b])
            copy.start()
            copies.append(copy)
    for b in range(half):
        pair = pl.ds(2 * b, 2)
        pltpu.make_async_copy(dq_out.at[pair], dq_ref.at[pair], sem.at[b]).wait()
    for copy in copies:
        copy.wait()


def attention(upper, kv_own, kv_low, qd, gain):
    parts, twice, rows, width = qd.shape
    layers = twice // 2
    kv_width = kv_own.shape[2]
    half = parts // 2
    size = 2 * rows
    stack = layers * (width // HD) * size
    return pl.pallas_call(
        attention_kernel,
        out_shape=(
            jax.ShapeDtypeStruct((parts, layers, rows, width), BF16),
            jax.ShapeDtypeStruct((parts, 2 * rows, kv_width), F32),
            jax.ShapeDtypeStruct((parts, 2 * rows, kv_width), BF16),
            jax.ShapeDtypeStruct((8, HD), F32),
        ),
        in_specs=[pl.BlockSpec(memory_space=pltpu.SMEM)] + [whole()] * 4,
        out_specs=(in_hbm(),) * 3 + (whole(),),
        scratch_shapes=[
            pltpu.VMEM((2 * half, size, HD), BF16),
            pltpu.VMEM((2 * half, size, HD), BF16),
            pltpu.VMEM((2 * half, HD, size), BF16),
            pltpu.VMEM((half, 1, size), F32),
            pltpu.VMEM((HD, stack), F32),
            pltpu.VMEM((1, stack), F32),
            pltpu.VMEM((HD, stack), BF16),
            pltpu.VMEM((stack, HD), BF16),
            pltpu.VMEM((half + 1, size, stack), F32),
            pltpu.VMEM((half + 1, size, stack), F32),
            pltpu.VMEM((half + 1, 1, stack), F32),
            pltpu.VMEM((width // HD, 2, 2 * half, size, HD), F32),
            pltpu.VMEM((HD, stack), F32),
            pltpu.VMEM((layers, HD, rows), F32),
            pltpu.VMEM((parts, layers, rows, width), BF16),
            pltpu.VMEM((parts, 2 * rows, kv_width), F32),
            pltpu.VMEM((parts, 2 * rows, kv_width), BF16),
            pltpu.SemaphoreType.DMA((3 * half,)),
        ],
        compiler_params=params(52),
        name="attention",
    )(upper, kv_own, kv_low, qd, gain)


RING = 4


def pair_sum(x, axis, perm):
    return x + lax.ppermute(x, axis, perm)


def ring_sum(x, axis, shift):
    one, two, three = (lax.ppermute(x, axis, shift(k)) for k in (1, 2, 3))
    return (x + two) + (one + three)


def over_x(x):
    return ring_sum(
        x,
        "dp",
        lambda k: [
            (d, d // RING * RING + (d + k) % RING) for d in range(lax.axis_size("dp"))
        ],
    )


def over_z(x):
    n_sp, n_dp = lax.axis_size("sp"), lax.axis_size("dp")
    x = ring_sum(x, "dp", lambda k: [(d, (d + k * RING) % n_dp) for d in range(n_dp)])
    return pair_sum(x, "sp", [(s, (s + n_sp // 2) % n_sp) for s in range(n_sp)])


def on_device(queries, dout, keys, values, gain, segments):
    layers, _, rows, channels = queries.shape
    n_sp = lax.axis_size("sp")
    parts = n_sp // 2
    groups = [list(range(parts)), list(range(parts, n_sp))]
    low_to_up = [(s, s + parts) for s in range(parts)]
    up_to_low = [(s + parts, s) for s in range(parts)]
    width = channels // parts
    kv_width = keys.shape[2] // parts
    upper = (lax.axis_index("sp") >= parts).astype(jnp.int32).reshape(1)

    def exchange(x):
        return lax.all_to_all(x, "sp", 0, 0, axis_index_groups=groups, tiled=True)

    kv_send = pl.pallas_call(
        pack_kv_kernel,
        out_shape=jax.ShapeDtypeStruct((parts, 2 * rows + IDS, kv_width), BF16),
        in_specs=[whole()] * 3,
        out_specs=whole(),
        compiler_params=params(63),
        name="pack_kv",
    )(keys[0], values[0], segments)
    kv_own = exchange(kv_send)
    queries, dout, _ = lax.optimization_barrier((queries, dout, kv_send))
    qd_send = pl.pallas_call(
        pack_q_kernel,
        out_shape=jax.ShapeDtypeStruct((parts, 2 * layers, rows, width), BF16),
        in_specs=[whole()] * 2,
        out_specs=whole(),
        compiler_params=params(63),
        name="pack_q",
    )(queries[:, 0], dout[:, 0])
    kv_low = lax.ppermute(kv_own, "sp", low_to_up)
    qd = exchange(qd_send)

    dq_send, kv_sum, cross, dgain = attention(upper, kv_own, kv_low, qd, gain)

    cross_low = lax.ppermute(cross, "sp", up_to_low)
    dgain = over_x(dgain)
    dq_recv = exchange(dq_send)
    dgain = over_z(dgain)
    kv_out = pl.pallas_call(
        combine_kernel,
        out_shape=jax.ShapeDtypeStruct(
            (parts, 2 * rows + (PIECES + 1) * GAIN_ROWS, kv_width), BF16
        ),
        in_specs=[whole()] * 3,
        out_specs=whole(),
        compiler_params=params(16),
        name="combine",
    )(kv_sum, cross_low, dgain)
    dkv_recv = exchange(kv_out)
    dqueries = pl.pallas_call(
        unpack_q_kernel,
        out_shape=jax.ShapeDtypeStruct((layers, rows, channels), BF16),
        in_specs=[whole()],
        out_specs=whole(),
        compiler_params=params(16),
        name="unpack_q",
    )(dq_recv)
    dkeys, dvalues, dgain = pl.pallas_call(
        unpack_kv_kernel,
        out_shape=(jax.ShapeDtypeStruct((rows, keys.shape[2]), BF16),) * 2
        + (jax.ShapeDtypeStruct(gain.shape, F32),),
        in_specs=[whole()],
        out_specs=(whole(),) * 3,
        compiler_params=params(16),
        name="unpack_kv",
    )(dkv_recv)
    return dqueries[:, None], dkeys[None], dvalues[None], dgain


def solution(mesh):
    return jax.shard_map(
        on_device,
        mesh=mesh,
        in_specs=(
            P(None, "dp", "sp", None),
            P(None, "dp", "sp", None),
            P("dp", "sp", None),
            P("dp", "sp", None),
            P(),
            P("dp", "sp"),
        ),
        out_specs=(P(None, "dp", "sp", None), P("dp", "sp", None), P("dp", "sp", None), P()),
        check_vma=False,
    )
```

time: 136 us -> 133 us (0.978); the launches traced: 134 us -> 133 us
  waiting for transfers between devices: 48.7 us -> 39.8 us
  Pallas kernels: 19.1 us -> 27.8 us
  local copies, waits for them, and re-layouts: 7.37 us -> 0.81 us
  starting transfers between devices: 58.2 us -> 63.7 us
    ppermute x11 -> x7, waiting for transfers between devices: 16.8 us -> 5.49 us  [the longest x6 4.5 us: ring_sum(): one, two, three = (lax.ppermute(x, axis, shift(k)) for k in (1, 2, 3))]
    all_to_all x4, waiting for transfers between devices: 14.7 us -> 22.5 us  [exchange(): return lax.all_to_all(x, 'sp', 0, 0, axis_index_groups=groups, tiled=True)]
    ppermute x1, waiting for transfers between devices: 6.04 us -> 0.01 us  [on_device(): cross_low = lax.ppermute(cross, 'sp', up_to_low)]
    unnamed x24 -> x8, local copies, waits for them, and re-layouts: 6.81 us -> 0.81 us
    ppermute x11 -> x7, starting transfers between devices: 27.3 us -> 32 us  [the longest x1 20 us: pair_sum(): return x + lax.ppermute(x, axis, perm)]
    pallas_call x1, Pallas kernels: 15.1 us -> 19.9 us  [attention(): pl.pallas_call(attention_kernel, out_shape=(jax.ShapeDtypeStruct((parts,...]
    pallas_call x1, Pallas kernels: 0.16 us -> 3 us  [on_device(): pl.pallas_call(pack_q_kernel, out_shape=jax.ShapeDtypeStruct((parts, 2 *...]
    all_to_all x4, starting transfers between devices: 20.8 us -> 22.3 us  [exchange(): return lax.all_to_all(x, 'sp', 0, 0, axis_index_groups=groups, tiled=True)]
  transfers between devices with their start and end apart: 17 -> 13, of which waited for: 10 -> 9; matrix products, arithmetic and copies ran while one was open for 0% -> 0% of each run, Pallas kernels for 2% -> 4%
where the time goes in v2:
time: 133 us
  starting transfers between devices  63.7 us (48%)
  waiting for transfers between devices  39.8 us (30%)
  Pallas kernels  27.8 us (21%)
    all_to_all x4, waiting for transfers between devices, exchange(): return lax.all_to_all(x, 'sp', 0, 0, axis_index_groups=groups, tiled=True)  22.5 us
    all_to_all x4, starting transfers between devices, exchange(): return lax.all_to_all(x, 'sp', 0, 0, axis_index_groups=groups, tiled=True)  22.3 us
    ppermute x1, starting transfers between devices, pair_sum(): return x + lax.ppermute(x, axis, perm)  20 us
    pallas_call x1, Pallas kernels, attention(): pl.pallas_call(attention_kernel, out_shape=(jax.ShapeDtypeStruct((parts,...  19.9 us
    ppermute x6, starting transfers between devices, ring_sum(): one, two, three = (lax.ppermute(x, axis, shift(k)) for k in (1, 2, 3))  12 us
    ppermute x1, waiting for transfers between devices, on_device(): kv_low = lax.ppermute(kv_own, 'sp', low_to_up)  11.8 us
    ppermute x1, starting transfers between devices, on_device(): kv_low = lax.ppermute(kv_own, 'sp', low_to_up)  8.11 us
    ppermute x6, waiting for transfers between devices, ring_sum(): one, two, three = (lax.ppermute(x, axis, shift(k)) for k in (1, 2, 3))  4.5 us
  transfers between devices with their start and end apart: 13, of which 9 were waited for; matrix products, arithmetic and copies ran while one was open for 0% of the time, Pallas kernels for 4%

profile of v2, /device:TPU:1, one launch (start us, length us, event | category | flops | bytes accessed | tf_op | source)
XLA Modules:
  0.0 132.8 jit_solution(1910994133950100950)
XLA Ops:
  0.6 1.9 %pack_kv.1 = bf16[8,272,128]{2,1,0:T(8,128)(2,1)} custom-call(bf16[128,1024]{1,0:T(8,128)(2,1)} %bitcast.13, bf16[128,1024]{1,0:T(8,128)(2,1)} %bitcast.14, s32[1,128]{1,0:T(1,128)} %seg_ref.1), custom_call_target="tpu_custom_call" | custom-call | tf_op jit(solution)/shard_map/pack_kv/pallas_call | solution.py:376
  2.6 6.7 %all-to-all-start = ((bf16[8,272,128]{2,1,0:T(8,128)(2,1)}), bf16[8,272,128]{2,1,0:T(8,128)(2,1)S(1)}, u32[]{:S(2)}, u32[]{:S(2)}) async-start(bf16[8,272,128]{2,1,0:T(8,128)(2,1)} %pack_kv.1), calls=%async_computation | async-start | bytes 1114112 | tf_op jit(solution)/shard_map/all_to_all | solution.py:374
  9.2 3.0 %pack_q.1 = bf16[8,4,128,256]{3,2,1,0:T(8,128)(2,1)} custom-call(bf16[2,128,2048]{2,1,0:T(8,128)(2,1)} %bitcast.11, bf16[2,128,2048]{2,1,0:T(8,128)(2,1)} %bitcast.12), custom_call_target="tpu_custom_call" | custom-call | tf_op jit(solution)/shard_map/pack_q/pallas_call | solution.py:386
  12.2 6.8 %all-to-all-done.own_kv_ref = bf16[8,272,128]{2,1,0:T(8,128)(2,1)S(1)} async-done(((bf16[8,272,128]{2,1,0:T(8,128)(2,1)}), bf16[8,272,128]{2,1,0:T(8,128)(2,1)S(1)}, u32[]{:S(2)}, u32[]{:S(2)}) %all-to-all-start) | async-done | bytes 557088 | tf_op jit(solution)/shard_map/all_to_all | solution.py:374
  19.1 5.1 %all-to-all-start.1 = ((bf16[8,4,128,256]{3,2,1,0:T(8,128)(2,1)}), bf16[8,4,128,256]{3,2,1,0:T(8,128)(2,1)}, u32[]{:S(2)}, u32[]{:S(2)}) async-start(bf16[8,4,128,256]{3,2,1,0:T(8,128)(2,1)} %pack_q.1), calls=%async_computation.1 | async-start | bytes 4194304 | tf_op jit(solution)/shard_map/all_to_all | solution.py:374
  24.2 8.1 %collective-permute-start = (bf16[8,272,128]{2,1,0:T(8,128)(2,1)S(1)}, bf16[8,272,128]{2,1,0:T(8,128)(2,1)S(1)}, u32[]{:S(2)}, u32[]{:S(2)}) collective-permute-start(bf16[8,272,128]{2,1,0:T(8,128)(2,1)S(1)} %all-to-all-done.own_kv_ref), channel_id=1, source_target_pairs={{0,8},{1,9},{2,10},{3,11},{4,12},{5,13},{6,14},{7,15},{16,24},{17,... | collective-permute-start | bytes 1671176 | tf_op jit(solution)/shard_map/ppermute | solution.py:394
  32.3 11.8 %collective-permute-done.low_kv_ref = bf16[8,272,128]{2,1,0:T(8,128)(2,1)S(1)} collective-permute-done((bf16[8,272,128]{2,1,0:T(8,128)(2,1)S(1)}, bf16[8,272,128]{2,1,0:T(8,128)(2,1)S(1)}, u32[]{:S(2)}, u32[]{:S(2)}) %collective-permute-start) | collective-permute-done | bytes 557088 | tf_op jit(solution)/shard_map/ppermute | solution.py:394
  44.1 6.5 %all-to-all-done.1.qd_ref = bf16[8,4,128,256]{3,2,1,0:T(8,128)(2,1)} async-done(((bf16[8,4,128,256]{3,2,1,0:T(8,128)(2,1)}), bf16[8,4,128,256]{3,2,1,0:T(8,128)(2,1)}, u32[]{:S(2)}, u32[]{:S(2)}) %all-to-all-start.1) | async-done | bytes 2097184 | tf_op jit(solution)/shard_map/all_to_all | solution.py:374
  50.6 19.9 %attention.1 = (bf16[8,2,128,256]{3,2,1,0:T(8,128)(2,1)}, f32[8,256,128]{2,1,0:T(8,128)}, bf16[8,256,128]{2,1,0:T(8,128)(2,1)S(1)}, f32[8,128]{1,0:T(8,128)S(1)}) custom-call(s32[1]{0:T(128)} %bitcast.upper_ref, bf16[8,272,128]{2,1,0:T(8,128)(2,1)S(1)} %all-to-all-done.own_kv_ref, bf16[8,272,128]{2,1,0:T(8,128)(2,1)S(1)} %collective-permute-done.low_kv_ref, ...), custom_call_target="tpu_custom_call" | custom-call | tf_op jit(solution)/shard_map/attention/pallas_call | solution.py:299
  70.6 0.8 copy-done.2
  71.4 4.5 %all-to-all-start.2 = ((bf16[8,2,128,256]{3,2,1,0:T(8,128)(2,1)}), bf16[8,2,128,256]{3,2,1,0:T(8,128)(2,1)S(1)}, u32[]{:S(2)}, u32[]{:S(2)}) async-start(bf16[8,2,128,256]{3,2,1,0:T(8,128)(2,1)} %get-tuple-element.15), calls=%async_computation.2 | async-start | bytes 2097152 | tf_op jit(solution)/shard_map/all_to_all | solution.py:374
  75.8 1.3 collective-permute-start.1
  77.1 1.8 %collective-permute-start.4 = (f32[8,128]{1,0:T(8,128)S(1)}, f32[8,128]{1,0:T(8,128)S(1)}, u32[]{:S(2)}, u32[]{:S(2)}) collective-permute-start(f32[8,128]{1,0:T(8,128)S(1)} %get-tuple-element.18), channel_id=1, source_target_pairs={{0,48},{16,0},{32,16},{48,32},{64,112},{80,64},{96,80},{112,96},{1... | collective-permute-start | bytes 12296 | tf_op jit(solution)/shard_map/ppermute | solution.py:342
  79.0 0.0 collective-permute-start.3
  79.0 1.3 collective-permute-start.2
  80.2 0.0 collective-permute-done.4
  80.2 2.4 %collective-permute-done.3 = f32[8,128]{1,0:T(8,128)S(1)} collective-permute-done((f32[8,128]{1,0:T(8,128)S(1)}, f32[8,128]{1,0:T(8,128)S(1)}, u32[]{:S(2)}, u32[]{:S(2)}) %collective-permute-start.3) | collective-permute-done | bytes 4128 | tf_op jit(solution)/shard_map/ppermute | solution.py:342
  82.6 0.3 collective-permute-done.2
  82.9 3.1 %collective-permute-start.7 = (f32[8,128]{1,0:T(8,128)S(1)}, f32[8,128]{1,0:T(8,128)S(1)}, u32[]{:S(2)}, u32[]{:S(2)}) collective-permute-start(f32[8,128]{1,0:T(8,128)S(1)} %add_add_fusion.1), channel_id=1, source_target_pairs={{0,192},{16,208},{32,224},{48,240},{64,0},{80,16},{96,32},{112,48}... | collective-permute-start | bytes 12296 | tf_op jit(solution)/shard_map/ppermute | solution.py:342
  86.1 3.9 %collective-permute-start.6 = (f32[8,128]{1,0:T(8,128)S(1)}, f32[8,128]{1,0:T(8,128)S(1)}, u32[]{:S(2)}, u32[]{:S(2)}) collective-permute-start(f32[8,128]{1,0:T(8,128)S(1)} %add_add_fusion.1), channel_id=1, source_target_pairs={{0,64},{16,80},{32,96},{48,112},{64,128},{80,144},{96,160},{112,17... | collective-permute-start | bytes 12296 | tf_op jit(solution)/shard_map/ppermute | solution.py:342
  90.0 1.8 %collective-permute-start.5 = (f32[8,128]{1,0:T(8,128)S(1)}, f32[8,128]{1,0:T(8,128)S(1)}, u32[]{:S(2)}, u32[]{:S(2)}) collective-permute-start(f32[8,128]{1,0:T(8,128)S(1)} %add_add_fusion.1), channel_id=1, source_target_pairs={{0,128},{16,144},{32,160},{48,176},{64,192},{80,208},{96,224},{112... | collective-permute-start | bytes 12296 | tf_op jit(solution)/shard_map/ppermute | solution.py:342
  91.8 0.0 collective-permute-done.7
  91.8 1.0 collective-permute-done.6
  92.9 0.8 collective-permute-done.5
  93.6 20.0 %collective-permute-start.8 = (f32[8,128]{1,0:T(8,128)S(1)}, f32[8,128]{1,0:T(8,128)S(1)}, u32[]{:S(2)}, u32[]{:S(2)}) collective-permute-start(f32[8,128]{1,0:T(8,128)S(1)} %add_add_fusion), channel_id=1, source_target_pairs={{0,8},{1,9},{2,10},{3,11},{4,12},{5,13},{6,14},{7,15},{8,0},{9,1},... | collective-permute-start | bytes 12296 | tf_op jit(solution)/shard_map/ppermute | solution.py:338
  113.7 1.0 collective-permute-done.8
  114.7 0.9 combine.1
  115.6 0.0 all-to-all-done.2.in_ref
  115.6 6.1 %all-to-all-start.3 = ((bf16[8,288,128]{2,1,0:T(8,128)(2,1)}), bf16[8,288,128]{2,1,0:T(8,128)(2,1)S(1)}, u32[]{:S(2)}, u32[]{:S(2)}) async-start(bf16[8,288,128]{2,1,0:T(8,128)(2,1)} %combine.1), calls=%async_computation.3 | async-start | bytes 1179648 | tf_op jit(solution)/shard_map/all_to_all | solution.py:374
  121.7 1.1 unpack_q.1
  122.8 9.1 %all-to-all-done.3.in_ref = bf16[8,288,128]{2,1,0:T(8,128)(2,1)S(1)} async-done(((bf16[8,288,128]{2,1,0:T(8,128)(2,1)}), bf16[8,288,128]{2,1,0:T(8,128)(2,1)S(1)}, u32[]{:S(2)}, u32[]{:S(2)}) %all-to-all-start.3) | async-done | bytes 589856 | tf_op jit(solution)/shard_map/all_to_all | solution.py:374
  131.8 0.9 unpack_kv.1
  (11 shorter events, 0.0 us)
Async XLA Ops:
  2.6 16.5 %all-to-all-start = ((bf16[8,272,128]{2,1,0:T(8,128)(2,1)}), bf16[8,272,128]{2,1,0:T(8,128)(2,1)S(1)}, u32[]{:S(2)}, u32[]{:S(2)}) async-start(bf16[8,272,128]{2,1,0:T(8,128)(2,1)} %pack_kv.1), calls=%async_computation | async-start | bytes 1114112 | tf_op jit(solution)/shard_map/all_to_all | solution.py:374
  12.2 38.4 %copy-start.1 = (f32[2,128]{1,0:T(2,128)S(1)}, f32[2,128]{1,0:T(2,128)}, u32[]{:S(2)}) copy-start(f32[2,128]{1,0:T(2,128)} %gain_ref.1) | copy-start | bytes 3076
  19.1 31.5 %all-to-all-start.1 = ((bf16[8,4,128,256]{3,2,1,0:T(8,128)(2,1)}), bf16[8,4,128,256]{3,2,1,0:T(8,128)(2,1)}, u32[]{:S(2)}, u32[]{:S(2)}) async-start(bf16[8,4,128,256]{3,2,1,0:T(8,128)(2,1)} %pack_q.1), calls=%async_computation.1 | async-start | bytes 4194304 | tf_op jit(solution)/shard_map/all_to_all | solution.py:374
  24.2 19.9 %collective-permute-start = (bf16[8,272,128]{2,1,0:T(8,128)(2,1)S(1)}, bf16[8,272,128]{2,1,0:T(8,128)(2,1)S(1)}, u32[]{:S(2)}, u32[]{:S(2)}) collective-permute-start(bf16[8,272,128]{2,1,0:T(8,128)(2,1)S(1)} %all-to-all-done.own_kv_ref), channel_id=1, source_target_pairs={{0,8},{1,9},{2,10},{3,11},{4,12},{5,13},{6,14},{7,15},{16,24},{17,... | collective-permute-start | bytes 1671176 | tf_op jit(solution)/shard_map/ppermute | solution.py:394
  70.6 0.8 copy-start.2
  71.4 43.3 %copy-start = (f32[8,256,128]{2,1,0:T(8,128)S(1)}, f32[8,256,128]{2,1,0:T(8,128)}, u32[]{:S(2)}) copy-start(f32[8,256,128]{2,1,0:T(8,128)} %get-tuple-element.16.own_ref) | copy-start | bytes 3145732
  71.4 4.5 %copy-start.3 = (bf16[8,256,128]{2,1,0:T(8,128)(2,1)S(1)}, bf16[8,256,128]{2,1,0:T(8,128)(2,1)}, u32[]{:S(2)}) copy-start(bf16[8,256,128]{2,1,0:T(8,128)(2,1)} %copy-done.2) | copy-start | bytes 1572868
  71.4 44.2 %all-to-all-start.2 = ((bf16[8,2,128,256]{3,2,1,0:T(8,128)(2,1)}), bf16[8,2,128,256]{3,2,1,0:T(8,128)(2,1)S(1)}, u32[]{:S(2)}, u32[]{:S(2)}) async-start(bf16[8,2,128,256]{3,2,1,0:T(8,128)(2,1)} %get-tuple-element.15), calls=%async_computation.2 | async-start | bytes 2097152 | tf_op jit(solution)/shard_map/all_to_all | solution.py:374
  75.8 38.8 %collective-permute-start.1 = (bf16[8,256,128]{2,1,0:T(8,128)(2,1)S(1)}, bf16[8,256,128]{2,1,0:T(8,128)(2,1)S(1)}, u32[]{:S(2)}, u32[]{:S(2)}) collective-permute-start(bf16[8,256,128]{2,1,0:T(8,128)(2,1)S(1)} %copy-done.3), channel_id=1, source_target_pairs={{8,0},{9,1},{10,2},{11,3},{12,4},{13,5},{14,6},{15,7},{24,16},{25,... | collective-permute-start | bytes 1572872 | tf_op jit(solution)/shard_map/ppermute | solution.py:399
  77.1 3.1 %collective-permute-start.4 = (f32[8,128]{1,0:T(8,128)S(1)}, f32[8,128]{1,0:T(8,128)S(1)}, u32[]{:S(2)}, u32[]{:S(2)}) collective-permute-start(f32[8,128]{1,0:T(8,128)S(1)} %get-tuple-element.18), channel_id=1, source_target_pairs={{0,48},{16,0},{32,16},{48,32},{64,112},{80,64},{96,80},{112,96},{1... | collective-permute-start | bytes 12296 | tf_op jit(solution)/shard_map/ppermute | solution.py:342
  79.0 3.7 %collective-permute-start.3 = (f32[8,128]{1,0:T(8,128)S(1)}, f32[8,128]{1,0:T(8,128)S(1)}, u32[]{:S(2)}, u32[]{:S(2)}) collective-permute-start(f32[8,128]{1,0:T(8,128)S(1)} %get-tuple-element.18), channel_id=1, source_target_pairs={{0,16},{16,32},{32,48},{48,0},{64,80},{80,96},{96,112},{112,64},{1... | collective-permute-start | bytes 12296 | tf_op jit(solution)/shard_map/ppermute | solution.py:342
  79.0 4.0 %collective-permute-start.2 = (f32[8,128]{1,0:T(8,128)S(1)}, f32[8,128]{1,0:T(8,128)S(1)}, u32[]{:S(2)}, u32[]{:S(2)}) collective-permute-start(f32[8,128]{1,0:T(8,128)S(1)} %get-tuple-element.18), channel_id=1, source_target_pairs={{0,32},{16,48},{32,0},{48,16},{64,96},{80,112},{96,64},{112,80},{1... | collective-permute-start | bytes 12296 | tf_op jit(solution)/shard_map/ppermute | solution.py:342
  82.9 8.9 %collective-permute-start.7 = (f32[8,128]{1,0:T(8,128)S(1)}, f32[8,128]{1,0:T(8,128)S(1)}, u32[]{:S(2)}, u32[]{:S(2)}) collective-permute-start(f32[8,128]{1,0:T(8,128)S(1)} %add_add_fusion.1), channel_id=1, source_target_pairs={{0,192},{16,208},{32,224},{48,240},{64,0},{80,16},{96,32},{112,48}... | collective-permute-start | bytes 12296 | tf_op jit(solution)/shard_map/ppermute | solution.py:342
  86.1 6.8 %collective-permute-start.6 = (f32[8,128]{1,0:T(8,128)S(1)}, f32[8,128]{1,0:T(8,128)S(1)}, u32[]{:S(2)}, u32[]{:S(2)}) collective-permute-start(f32[8,128]{1,0:T(8,128)S(1)} %add_add_fusion.1), channel_id=1, source_target_pairs={{0,64},{16,80},{32,96},{48,112},{64,128},{80,144},{96,160},{112,17... | collective-permute-start | bytes 12296 | tf_op jit(solution)/shard_map/ppermute | solution.py:342
  90.0 3.7 %collective-permute-start.5 = (f32[8,128]{1,0:T(8,128)S(1)}, f32[8,128]{1,0:T(8,128)S(1)}, u32[]{:S(2)}, u32[]{:S(2)}) collective-permute-start(f32[8,128]{1,0:T(8,128)S(1)} %add_add_fusion.1), channel_id=1, source_target_pairs={{0,128},{16,144},{32,160},{48,176},{64,192},{80,208},{96,224},{112... | collective-permute-start | bytes 12296 | tf_op jit(solution)/shard_map/ppermute | solution.py:342
  93.6 21.0 %collective-permute-start.8 = (f32[8,128]{1,0:T(8,128)S(1)}, f32[8,128]{1,0:T(8,128)S(1)}, u32[]{:S(2)}, u32[]{:S(2)}) collective-permute-start(f32[8,128]{1,0:T(8,128)S(1)} %add_add_fusion), channel_id=1, source_target_pairs={{0,8},{1,9},{2,10},{3,11},{4,12},{5,13},{6,14},{7,15},{8,0},{9,1},... | collective-permute-start | bytes 12296 | tf_op jit(solution)/shard_map/ppermute | solution.py:338
  115.6 16.2 %all-to-all-start.3 = ((bf16[8,288,128]{2,1,0:T(8,128)(2,1)}), bf16[8,288,128]{2,1,0:T(8,128)(2,1)S(1)}, u32[]{:S(2)}, u32[]{:S(2)}) async-start(bf16[8,288,128]{2,1,0:T(8,128)(2,1)} %combine.1), calls=%async_computation.3 | async-start | bytes 1179648 | tf_op jit(solution)/shard_map/all_to_all | solution.py:374

commit v3 on v2

--- a/solution.py
+++ b/solution.py
@@ -90,7 +90,7 @@
     upper_ref,
     own_kv_ref,
     low_kv_ref,
-    qd_ref,
+    qd_hbm,
     gain_ref,
     dq_ref,
     own_ref,
@@ -107,9 +107,13 @@
     expo,
     dprob,
     tops,
-    acc,
+    acc_k,
+    acc_v,
     dq_t,
     gain_acc,
+    first_all,
+    qd_ref,
+    qd_sem,
     dq_out,
     own_out,
     cross_out,
@@ -135,8 +139,14 @@
     def dot(a, b, dims):
         return lax.dot_general(a, b, dims, preferred_element_type=F32)
 
+    def load(i):
+        pair = pl.ds(2 * i, 2)
+        return pltpu.make_async_copy(qd_hbm.at[pair], qd_ref.at[pair], qd_sem.at[i])
+
+    for i in range(half):
+        load(i).start()
+
     unit = eye(HD).astype(BF16)
-    unit_size = eye(size).astype(BF16)
     gain_cols = [
         jnp.sum(eye(HD) * gain_ref[layer : layer + 1, :], axis=1, keepdims=True)
         for layer in range(layers)
@@ -165,8 +175,10 @@
         begin = jnp.where(ids_own == doc, total, begin)
     for b in range(half):
         start_all[b] = jnp.concatenate([begin[2 * b : 2 * b + 1], begin[2 * b + 1 : 2 * b + 2]], 1)
-
-    acc[...] = jnp.zeros_like(acc)
+        first_all[b] = jnp.min(begin[2 * b : 2 * b + 1]).astype(jnp.int32) // size
+
+    acc_k[...] = jnp.zeros_like(acc_k)
+    acc_v[...] = jnp.zeros_like(acc_v)
     gain_acc[...] = jnp.zeros_like(gain_acc)
 
     def part_of(i, layer, h, offset):
@@ -176,8 +188,11 @@
         )
 
     def q_block(i, carry):
+        load(i).wait()
+        q_all = jnp.concatenate([part_of(i, layer, h, 0) for _, h, layer in chunks], 0)
+        q_all = dot(unit, q_all, NT)
         for at, h, layer in chunks:
-            q = dot(unit, part_of(i, layer, h, 0), NT)
+            q = q_all[:, at]
             inv = lax.rsqrt(jnp.mean(q * q, axis=0, keepdims=True) + 1e-6)
             qhat = q * inv
             inv_row[:, at] = inv
@@ -185,18 +200,21 @@
             normed_t[:, at] = (qhat * gain_cols[layer]).astype(BF16)
             dout[at, :] = part_of(i, layer, h, layers)
         begin_row = start_all[i]
-        first = jnp.min(begin_row).astype(jnp.int32) // size
+        first = first_all[i]
         last = half + i
         count = last - first + 1
         begin_int = begin_row.astype(jnp.int32)
         token = last * size + lax.broadcasted_iota(jnp.int32, (1, size), 1)
         dq_t[...] = jnp.zeros_like(dq_t)
 
-        def sums(j, carry):
+        def sums(j, n, carry):
             kb = first + j
             k, v = k_all[kb], v_all[kb]
             u = kb * size + lax.broadcasted_iota(jnp.int32, (size, size), 0)
-            bias = jnp.where((u >= begin_int) & (u <= token), 0.0, -1e30)
+            allowed = u >= begin_int
+            if j == n - 1:
+                allowed = allowed & (u <= token)
+            bias = jnp.where(allowed, 0.0, -1e30)
             out = []
             for (at, _, _), (top, total, weighted) in zip(chunks, carry):
                 s = dot(k, normed_t[:, at], NN) + bias
@@ -218,30 +236,32 @@
 
         zero = jnp.zeros((1, size), F32)
         low = jnp.full((1, size), -1e30, F32)
-        stats = lax.fori_loop(0, count, sums, ((low, zero, zero),) * len(chunks))
-        shares = [1.0 / total for _, total, _ in stats]
-        deltas = [weighted * share for (_, _, weighted), share in zip(stats, shares)]
-
-        def grads(j, carry):
-            kb = first + j
-            kt = kt_all[kb]
-            probs, scores = [], []
-            for (at, _, _), (top, _, _), share, delta in zip(chunks, stats, shares, deltas):
-                prob = expo[j, :, at] * (share * jnp.exp2((tops[j, :, at] - top) * rate))
-                ds = (prob * ((dprob[j, :, at] - delta) * scale)).astype(BF16)
-                probs.append(prob.astype(BF16))
-                scores.append(ds)
-                dq_t[:, at] += dot(kt, ds, NN)
-            for h in range(group):
-                at = slice(h * layers * size, (h + 1) * layers * size)
-                mine = slice(h * layers, (h + 1) * layers)
-                ds = jnp.concatenate(scores[mine], 1)
-                prob = jnp.concatenate(probs[mine], 1)
-                acc[h, 0, kb] += dot(ds, normed_t[:, at], NT)
-                acc[h, 1, kb] += dot(prob, dout[at, :], NN)
-            return carry
-
-        lax.fori_loop(0, count, grads, 0)
+        def run(n):
+            stats = ((low, zero, zero),) * len(chunks)
+            for j in range(n):
+                stats = sums(j, n, stats)
+            shares = [1.0 / total for _, total, _ in stats]
+            deltas = [weighted * share for (_, _, weighted), share in zip(stats, shares)]
+
+            def grads(j, carry):
+                kb = first + j
+                kt = kt_all[kb]
+                probs, scores = [], []
+                for (at, _, _), (top, _, _), share, delta in zip(chunks, stats, shares, deltas):
+                    prob = expo[j, :, at] * (share * jnp.exp2((tops[j, :, at] - top) * rate))
+                    ds = (prob * ((dprob[j, :, at] - delta) * scale)).astype(BF16)
+                    probs.append(prob.astype(BF16))
+                    scores.append(ds)
+                    dq_t[:, at] += dot(kt, ds, NN)
+                acc_k[kb] += dot(jnp.concatenate(scores, 1), normed_t[...], NT)
+                acc_v[kb] += dot(jnp.concatenate(probs, 1), dout[...], NN)
+                return carry
+
+            for j in range(n):
+                grads(j, 0)
+
+        for n in range(1, half + 2):
+            pl.when(count == n)(functools.partial(run, n))
 
         for at, h, layer in chunks:
             dnorm, qhat = dq_t[:, at], qhat_t[:, at]
@@ -249,7 +269,7 @@
             gain_acc[layer] += part[:, :rows] + part[:, rows:]
             g = dnorm * gain_cols[layer]
             dq = inv_row[:, at] * (g - qhat * jnp.mean(g * qhat, axis=0, keepdims=True))
-            dq = dot(unit_size, dq.astype(BF16), NT).astype(BF16)
+            dq = dq.T.astype(BF16)
             cols = slice(h * HD, (h + 1) * HD)
             for j in range(2):
                 dq_out[2 * i + j, layer, :, cols] = dq[j * rows : (j + 1) * rows]
@@ -266,17 +286,10 @@
     for b in range(half):
         for j in range(2):
             part = slice(j * rows, (j + 1) * rows)
-            for kv in range(2):
+            for kv, acc in enumerate((acc_k, acc_v)):
                 out = slice(kv * rows, (kv + 1) * rows)
-                whole_sum = acc[0, kv, b, part, :]
-                own = acc[0, kv, half + b, part, :]
-                rounded = own.astype(BF16).astype(F32)
-                for h in range(1, group):
-                    whole_sum = whole_sum + acc[h, kv, b, part, :]
-                    own = own + acc[h, kv, half + b, part, :]
-                    rounded = rounded + acc[h, kv, half + b, part, :].astype(BF16).astype(F32)
-                cross_out[2 * b + j, out, :] = whole_sum.astype(BF16)
-                own_out[2 * b + j, out, :] = jnp.where(upper, rounded, own)
+                cross_out[2 * b + j, out, :] = acc[b, part, :].astype(BF16)
+                own_out[2 * b + j, out, :] = acc[half + b, part, :]
         pair = pl.ds(2 * b, 2)
         for n, (src, dst) in enumerate(((cross_out, cross_ref), (own_out, own_ref))):
             copy = pltpu.make_async_copy(src.at[pair], dst.at[pair], sem.at[half * (n + 1) + b])
@@ -304,7 +317,7 @@
             jax.ShapeDtypeStruct((parts, 2 * rows, kv_width), BF16),
             jax.ShapeDtypeStruct((8, HD), F32),
         ),
-        in_specs=[pl.BlockSpec(memory_space=pltpu.SMEM)] + [whole()] * 4,
+        in_specs=[pl.BlockSpec(memory_space=pltpu.SMEM), whole(), whole(), in_hbm(), whole()],
         out_specs=(in_hbm(),) * 3 + (whole(),),
         scratch_shapes=[
             pltpu.VMEM((2 * half, size, HD), BF16),
@@ -318,9 +331,13 @@
             pltpu.VMEM((half + 1, size, stack), F32),
             pltpu.VMEM((half + 1, size, stack), F32),
             pltpu.VMEM((half + 1, 1, stack), F32),
-            pltpu.VMEM((width // HD, 2, 2 * half, size, HD), F32),
+            pltpu.VMEM((2 * half, size, HD), F32),
+            pltpu.VMEM((2 * half, size, HD), F32),
             pltpu.VMEM((HD, stack), F32),
             pltpu.VMEM((layers, HD, rows), F32),
+            pltpu.SMEM((half,), jnp.int32),
+            pltpu.VMEM((parts, twice, rows, width), BF16),
+            pltpu.SemaphoreType.DMA((half,)),
             pltpu.VMEM((parts, layers, rows, width), BF16),
             pltpu.VMEM((parts, 2 * rows, kv_width), F32),
             pltpu.VMEM((parts, 2 * rows, kv_width), BF16),

time: 133 us -> 128 us (0.962); the launches traced: 133 us -> 126 us
  Pallas kernels: 27.8 us -> 21.9 us
    pallas_call x1, Pallas kernels: 19.9 us -> 14 us  [attention(): pl.pallas_call(attention_kernel, out_shape=(jax.ShapeDtypeStruct((parts,...]
    ppermute x1, starting transfers between devices: 20 us -> 16.8 us  [pair_sum(): return x + lax.ppermute(x, axis, perm)]
    ppermute x6, starting transfers between devices: 12 us -> 14.5 us  [ring_sum(): one, two, three = (lax.ppermute(x, axis, shift(k)) for k in (1, 2, 3))]
  transfers between devices with their start and end apart: 13 -> 13, of which waited for: 9 -> 8; matrix products, arithmetic and copies ran while one was open for 0% -> 0% of each run, Pallas kernels for 4% -> 4%
where the time goes in v3:
time: 128 us; the launch traced here: 126 us
  starting transfers between devices  63 us (49%)
  waiting for transfers between devices  39.9 us (31%)
  Pallas kernels  21.9 us (17%)
    all_to_all x4, waiting for transfers between devices, exchange(): return lax.all_to_all(x, 'sp', 0, 0, axis_index_groups=groups, tiled=True)  22.5 us
    all_to_all x4, starting transfers between devices, exchange(): return lax.all_to_all(x, 'sp', 0, 0, axis_index_groups=groups, tiled=True)  22.3 us
    ppermute x1, starting transfers between devices, pair_sum(): return x + lax.ppermute(x, axis, perm)  16.8 us
    ppermute x6, starting transfers between devices, ring_sum(): one, two, three = (lax.ppermute(x, axis, shift(k)) for k in (1, 2, 3))  14.5 us
    pallas_call x1, Pallas kernels, attention(): pl.pallas_call(attention_kernel, out_shape=(jax.ShapeDtypeStruct((parts,...  14 us
    ppermute x1, waiting for transfers between devices, on_device(): kv_low = lax.ppermute(kv_own, 'sp', low_to_up)  11.8 us
    ppermute x1, starting transfers between devices, on_device(): kv_low = lax.ppermute(kv_own, 'sp', low_to_up)  8.11 us
    ppermute x6, waiting for transfers between devices, ring_sum(): one, two, three = (lax.ppermute(x, axis, shift(k)) for k in (1, 2, 3))  4.66 us
  transfers between devices with their start and end apart: 13, of which 8 were waited for; matrix products, arithmetic and copies ran while one was open for 0% of the time, Pallas kernels for 4%

profile of v3, /device:TPU:1, one launch (start us, length us, event | category | flops | bytes accessed | tf_op | source)
XLA Modules:
  0.0 126.3 jit_solution(6830392699600697378)
XLA Ops:
  0.6 1.9 %pack_kv.1 = bf16[8,272,128]{2,1,0:T(8,128)(2,1)} custom-call(bf16[128,1024]{1,0:T(8,128)(2,1)} %bitcast.13, bf16[128,1024]{1,0:T(8,128)(2,1)} %bitcast.14, s32[1,128]{1,0:T(1,128)} %seg_ref.1), custom_call_target="tpu_custom_call" | custom-call | tf_op jit(solution)/shard_map/pack_kv/pallas_call | solution.py:393
  2.6 6.7 %all-to-all-start = ((bf16[8,272,128]{2,1,0:T(8,128)(2,1)}), bf16[8,272,128]{2,1,0:T(8,128)(2,1)S(1)}, u32[]{:S(2)}, u32[]{:S(2)}) async-start(bf16[8,272,128]{2,1,0:T(8,128)(2,1)} %pack_kv.1), calls=%async_computation | async-start | bytes 1114112 | tf_op jit(solution)/shard_map/all_to_all | solution.py:391
  9.2 3.0 %pack_q.1 = bf16[8,4,128,256]{3,2,1,0:T(8,128)(2,1)} custom-call(bf16[2,128,2048]{2,1,0:T(8,128)(2,1)} %bitcast.11, bf16[2,128,2048]{2,1,0:T(8,128)(2,1)} %bitcast.12), custom_call_target="tpu_custom_call" | custom-call | tf_op jit(solution)/shard_map/pack_q/pallas_call | solution.py:403
  12.2 6.8 %all-to-all-done.own_kv_ref = bf16[8,272,128]{2,1,0:T(8,128)(2,1)S(1)} async-done(((bf16[8,272,128]{2,1,0:T(8,128)(2,1)}), bf16[8,272,128]{2,1,0:T(8,128)(2,1)S(1)}, u32[]{:S(2)}, u32[]{:S(2)}) %all-to-all-start) | async-done | bytes 557088 | tf_op jit(solution)/shard_map/all_to_all | solution.py:391
  19.1 5.1 %all-to-all-start.1 = ((bf16[8,4,128,256]{3,2,1,0:T(8,128)(2,1)}), bf16[8,4,128,256]{3,2,1,0:T(8,128)(2,1)}, u32[]{:S(2)}, u32[]{:S(2)}) async-start(bf16[8,4,128,256]{3,2,1,0:T(8,128)(2,1)} %pack_q.1), calls=%async_computation.1 | async-start | bytes 4194304 | tf_op jit(solution)/shard_map/all_to_all | solution.py:391
  24.2 8.1 %collective-permute-start = (bf16[8,272,128]{2,1,0:T(8,128)(2,1)S(1)}, bf16[8,272,128]{2,1,0:T(8,128)(2,1)S(1)}, u32[]{:S(2)}, u32[]{:S(2)}) collective-permute-start(bf16[8,272,128]{2,1,0:T(8,128)(2,1)S(1)} %all-to-all-done.own_kv_ref), channel_id=1, source_target_pairs={{0,8},{1,9},{2,10},{3,11},{4,12},{5,13},{6,14},{7,15},{16,24},{17,... | collective-permute-start | bytes 1671176 | tf_op jit(solution)/shard_map/ppermute | solution.py:411
  32.3 11.8 %collective-permute-done.low_kv_ref = bf16[8,272,128]{2,1,0:T(8,128)(2,1)S(1)} collective-permute-done((bf16[8,272,128]{2,1,0:T(8,128)(2,1)S(1)}, bf16[8,272,128]{2,1,0:T(8,128)(2,1)S(1)}, u32[]{:S(2)}, u32[]{:S(2)}) %collective-permute-start) | collective-permute-done | bytes 557088 | tf_op jit(solution)/shard_map/ppermute | solution.py:411
  44.1 6.5 %all-to-all-done.1.qd_hbm = bf16[8,4,128,256]{3,2,1,0:T(8,128)(2,1)} async-done(((bf16[8,4,128,256]{3,2,1,0:T(8,128)(2,1)}), bf16[8,4,128,256]{3,2,1,0:T(8,128)(2,1)}, u32[]{:S(2)}, u32[]{:S(2)}) %all-to-all-start.1) | async-done | bytes 2097184 | tf_op jit(solution)/shard_map/all_to_all | solution.py:391
  50.6 14.0 %attention.1 = (bf16[8,2,128,256]{3,2,1,0:T(8,128)(2,1)}, f32[8,256,128]{2,1,0:T(8,128)}, bf16[8,256,128]{2,1,0:T(8,128)(2,1)S(1)}, f32[8,128]{1,0:T(8,128)S(1)}) custom-call(s32[1]{0:T(128)} %bitcast.upper_ref, bf16[8,272,128]{2,1,0:T(8,128)(2,1)S(1)} %all-to-all-done.own_kv_ref, bf16[8,272,128]{2,1,0:T(8,128)(2,1)S(1)} %collective-permute-done.low_kv_ref, ...), custom_call_target="tpu_custom_call" | custom-call | tf_op jit(solution)/shard_map/attention/pallas_call | solution.py:312
  64.7 0.8 copy-done.2
  65.5 4.5 %all-to-all-start.2 = ((bf16[8,2,128,256]{3,2,1,0:T(8,128)(2,1)}), bf16[8,2,128,256]{3,2,1,0:T(8,128)(2,1)S(1)}, u32[]{:S(2)}, u32[]{:S(2)}) async-start(bf16[8,2,128,256]{3,2,1,0:T(8,128)(2,1)} %get-tuple-element.15), calls=%async_computation.2 | async-start | bytes 2097152 | tf_op jit(solution)/shard_map/all_to_all | solution.py:391
  70.0 1.3 %collective-permute-start.1 = (bf16[8,256,128]{2,1,0:T(8,128)(2,1)S(1)}, bf16[8,256,128]{2,1,0:T(8,128)(2,1)S(1)}, u32[]{:S(2)}, u32[]{:S(2)}) collective-permute-start(bf16[8,256,128]{2,1,0:T(8,128)(2,1)S(1)} %copy-done.3), channel_id=1, source_target_pairs={{8,0},{9,1},{10,2},{11,3},{12,4},{13,5},{14,6},{15,7},{24,16},{25,... | collective-permute-start | bytes 1572872 | tf_op jit(solution)/shard_map/ppermute | solution.py:416
  71.3 4.5 %collective-permute-start.4 = (f32[8,128]{1,0:T(8,128)S(1)}, f32[8,128]{1,0:T(8,128)S(1)}, u32[]{:S(2)}, u32[]{:S(2)}) collective-permute-start(f32[8,128]{1,0:T(8,128)S(1)} %get-tuple-element.18), channel_id=1, source_target_pairs={{0,48},{16,0},{32,16},{48,32},{64,112},{80,64},{96,80},{112,96},{1... | collective-permute-start | bytes 12296 | tf_op jit(solution)/shard_map/ppermute | solution.py:359
  75.7 0.0 collective-permute-start.3
  75.7 1.3 %collective-permute-start.2 = (f32[8,128]{1,0:T(8,128)S(1)}, f32[8,128]{1,0:T(8,128)S(1)}, u32[]{:S(2)}, u32[]{:S(2)}) collective-permute-start(f32[8,128]{1,0:T(8,128)S(1)} %get-tuple-element.18), channel_id=1, source_target_pairs={{0,32},{16,48},{32,0},{48,16},{64,96},{80,112},{96,64},{112,80},{1... | collective-permute-start | bytes 12296 | tf_op jit(solution)/shard_map/ppermute | solution.py:359
  77.0 0.0 collective-permute-done.4
  77.0 2.7 %collective-permute-done.3 = f32[8,128]{1,0:T(8,128)S(1)} collective-permute-done((f32[8,128]{1,0:T(8,128)S(1)}, f32[8,128]{1,0:T(8,128)S(1)}, u32[]{:S(2)}, u32[]{:S(2)}) %collective-permute-start.3) | collective-permute-done | bytes 4128 | tf_op jit(solution)/shard_map/ppermute | solution.py:359
  79.7 0.0 collective-permute-done.2
  79.7 3.3 %collective-permute-start.7 = (f32[8,128]{1,0:T(8,128)S(1)}, f32[8,128]{1,0:T(8,128)S(1)}, u32[]{:S(2)}, u32[]{:S(2)}) collective-permute-start(f32[8,128]{1,0:T(8,128)S(1)} %add_add_fusion.1), channel_id=1, source_target_pairs={{0,192},{16,208},{32,224},{48,240},{64,0},{80,16},{96,32},{112,48}... | collective-permute-start | bytes 12296 | tf_op jit(solution)/shard_map/ppermute | solution.py:359
  83.0 3.7 %collective-permute-start.6 = (f32[8,128]{1,0:T(8,128)S(1)}, f32[8,128]{1,0:T(8,128)S(1)}, u32[]{:S(2)}, u32[]{:S(2)}) collective-permute-start(f32[8,128]{1,0:T(8,128)S(1)} %add_add_fusion.1), channel_id=1, source_target_pairs={{0,64},{16,80},{32,96},{48,112},{64,128},{80,144},{96,160},{112,17... | collective-permute-start | bytes 12296 | tf_op jit(solution)/shard_map/ppermute | solution.py:359
  86.7 1.7 %collective-permute-start.5 = (f32[8,128]{1,0:T(8,128)S(1)}, f32[8,128]{1,0:T(8,128)S(1)}, u32[]{:S(2)}, u32[]{:S(2)}) collective-permute-start(f32[8,128]{1,0:T(8,128)S(1)} %add_add_fusion.1), channel_id=1, source_target_pairs={{0,128},{16,144},{32,160},{48,176},{64,192},{80,208},{96,224},{112... | collective-permute-start | bytes 12296 | tf_op jit(solution)/shard_map/ppermute | solution.py:359
  88.4 1.0 collective-permute-done.6
  89.5 0.9 collective-permute-done.5
  90.4 16.8 %collective-permute-start.8 = (f32[8,128]{1,0:T(8,128)S(1)}, f32[8,128]{1,0:T(8,128)S(1)}, u32[]{:S(2)}, u32[]{:S(2)}) collective-permute-start(f32[8,128]{1,0:T(8,128)S(1)} %add_add_fusion), channel_id=1, source_target_pairs={{0,8},{1,9},{2,10},{3,11},{4,12},{5,13},{6,14},{7,15},{8,0},{9,1},... | collective-permute-start | bytes 12296 | tf_op jit(solution)/shard_map/ppermute | solution.py:355
  107.2 1.0 collective-permute-done.8
  108.2 0.0 collective-permute-done.1.cross_ref
  108.2 0.9 combine.1
  109.1 0.0 all-to-all-done.2.in_ref
  109.1 6.1 %all-to-all-start.3 = ((bf16[8,288,128]{2,1,0:T(8,128)(2,1)}), bf16[8,288,128]{2,1,0:T(8,128)(2,1)S(1)}, u32[]{:S(2)}, u32[]{:S(2)}) async-start(bf16[8,288,128]{2,1,0:T(8,128)(2,1)} %combine.1), calls=%async_computation.3 | async-start | bytes 1179648 | tf_op jit(solution)/shard_map/all_to_all | solution.py:391
  115.2 1.1 unpack_q.1
  116.3 9.1 %all-to-all-done.3.in_ref = bf16[8,288,128]{2,1,0:T(8,128)(2,1)S(1)} async-done(((bf16[8,288,128]{2,1,0:T(8,128)(2,1)}), bf16[8,288,128]{2,1,0:T(8,128)(2,1)S(1)}, u32[]{:S(2)}, u32[]{:S(2)}) %all-to-all-start.3) | async-done | bytes 589856 | tf_op jit(solution)/shard_map/all_to_all | solution.py:391
  125.4 0.9 unpack_kv.1
  (11 shorter events, 0.0 us)
Async XLA Ops:
  2.6 16.5 %all-to-all-start = ((bf16[8,272,128]{2,1,0:T(8,128)(2,1)}), bf16[8,272,128]{2,1,0:T(8,128)(2,1)S(1)}, u32[]{:S(2)}, u32[]{:S(2)}) async-start(bf16[8,272,128]{2,1,0:T(8,128)(2,1)} %pack_kv.1), calls=%async_computation | async-start | bytes 1114112 | tf_op jit(solution)/shard_map/all_to_all | solution.py:391
  12.2 38.4 %copy-start.1 = (f32[2,128]{1,0:T(2,128)S(1)}, f32[2,128]{1,0:T(2,128)}, u32[]{:S(2)}) copy-start(f32[2,128]{1,0:T(2,128)} %gain_ref.1) | copy-start | bytes 3076
  19.1 31.5 %all-to-all-start.1 = ((bf16[8,4,128,256]{3,2,1,0:T(8,128)(2,1)}), bf16[8,4,128,256]{3,2,1,0:T(8,128)(2,1)}, u32[]{:S(2)}, u32[]{:S(2)}) async-start(bf16[8,4,128,256]{3,2,1,0:T(8,128)(2,1)} %pack_q.1), calls=%async_computation.1 | async-start | bytes 4194304 | tf_op jit(solution)/shard_map/all_to_all | solution.py:391
  24.2 19.9 %collective-permute-start = (bf16[8,272,128]{2,1,0:T(8,128)(2,1)S(1)}, bf16[8,272,128]{2,1,0:T(8,128)(2,1)S(1)}, u32[]{:S(2)}, u32[]{:S(2)}) collective-permute-start(bf16[8,272,128]{2,1,0:T(8,128)(2,1)S(1)} %all-to-all-done.own_kv_ref), channel_id=1, source_target_pairs={{0,8},{1,9},{2,10},{3,11},{4,12},{5,13},{6,14},{7,15},{16,24},{17,... | collective-permute-start | bytes 1671176 | tf_op jit(solution)/shard_map/ppermute | solution.py:411
  64.7 0.8 copy-start.2
  65.5 42.7 %copy-start = (f32[8,256,128]{2,1,0:T(8,128)S(1)}, f32[8,256,128]{2,1,0:T(8,128)}, u32[]{:S(2)}) copy-start(f32[8,256,128]{2,1,0:T(8,128)} %get-tuple-element.16.own_ref) | copy-start | bytes 3145732
  65.5 4.5 %copy-start.3 = (bf16[8,256,128]{2,1,0:T(8,128)(2,1)S(1)}, bf16[8,256,128]{2,1,0:T(8,128)(2,1)}, u32[]{:S(2)}) copy-start(bf16[8,256,128]{2,1,0:T(8,128)(2,1)} %copy-done.2) | copy-start | bytes 1572868
  65.5 43.7 %all-to-all-start.2 = ((bf16[8,2,128,256]{3,2,1,0:T(8,128)(2,1)}), bf16[8,2,128,256]{3,2,1,0:T(8,128)(2,1)S(1)}, u32[]{:S(2)}, u32[]{:S(2)}) async-start(bf16[8,2,128,256]{3,2,1,0:T(8,128)(2,1)} %get-tuple-element.15), calls=%async_computation.2 | async-start | bytes 2097152 | tf_op jit(solution)/shard_map/all_to_all | solution.py:391
  70.0 38.2 %collective-permute-start.1 = (bf16[8,256,128]{2,1,0:T(8,128)(2,1)S(1)}, bf16[8,256,128]{2,1,0:T(8,128)(2,1)S(1)}, u32[]{:S(2)}, u32[]{:S(2)}) collective-permute-start(bf16[8,256,128]{2,1,0:T(8,128)(2,1)S(1)} %copy-done.3), channel_id=1, source_target_pairs={{8,0},{9,1},{10,2},{11,3},{12,4},{13,5},{14,6},{15,7},{24,16},{25,... | collective-permute-start | bytes 1572872 | tf_op jit(solution)/shard_map/ppermute | solution.py:416
  71.3 5.7 %collective-permute-start.4 = (f32[8,128]{1,0:T(8,128)S(1)}, f32[8,128]{1,0:T(8,128)S(1)}, u32[]{:S(2)}, u32[]{:S(2)}) collective-permute-start(f32[8,128]{1,0:T(8,128)S(1)} %get-tuple-element.18), channel_id=1, source_target_pairs={{0,48},{16,0},{32,16},{48,32},{64,112},{80,64},{96,80},{112,96},{1... | collective-permute-start | bytes 12296 | tf_op jit(solution)/shard_map/ppermute | solution.py:359
  75.7 4.0 %collective-permute-start.3 = (f32[8,128]{1,0:T(8,128)S(1)}, f32[8,128]{1,0:T(8,128)S(1)}, u32[]{:S(2)}, u32[]{:S(2)}) collective-permute-start(f32[8,128]{1,0:T(8,128)S(1)} %get-tuple-element.18), channel_id=1, source_target_pairs={{0,16},{16,32},{32,48},{48,0},{64,80},{80,96},{96,112},{112,64},{1... | collective-permute-start | bytes 12296 | tf_op jit(solution)/shard_map/ppermute | solution.py:359
  75.7 4.0 %collective-permute-start.2 = (f32[8,128]{1,0:T(8,128)S(1)}, f32[8,128]{1,0:T(8,128)S(1)}, u32[]{:S(2)}, u32[]{:S(2)}) collective-permute-start(f32[8,128]{1,0:T(8,128)S(1)} %get-tuple-element.18), channel_id=1, source_target_pairs={{0,32},{16,48},{32,0},{48,16},{64,96},{80,112},{96,64},{112,80},{1... | collective-permute-start | bytes 12296 | tf_op jit(solution)/shard_map/ppermute | solution.py:359
  79.7 8.7 %collective-permute-start.7 = (f32[8,128]{1,0:T(8,128)S(1)}, f32[8,128]{1,0:T(8,128)S(1)}, u32[]{:S(2)}, u32[]{:S(2)}) collective-permute-start(f32[8,128]{1,0:T(8,128)S(1)} %add_add_fusion.1), channel_id=1, source_target_pairs={{0,192},{16,208},{32,224},{48,240},{64,0},{80,16},{96,32},{112,48}... | collective-permute-start | bytes 12296 | tf_op jit(solution)/shard_map/ppermute | solution.py:359
  83.0 6.4 %collective-permute-start.6 = (f32[8,128]{1,0:T(8,128)S(1)}, f32[8,128]{1,0:T(8,128)S(1)}, u32[]{:S(2)}, u32[]{:S(2)}) collective-permute-start(f32[8,128]{1,0:T(8,128)S(1)} %add_add_fusion.1), channel_id=1, source_target_pairs={{0,64},{16,80},{32,96},{48,112},{64,128},{80,144},{96,160},{112,17... | collective-permute-start | bytes 12296 | tf_op jit(solution)/shard_map/ppermute | solution.py:359
  86.7 3.7 %collective-permute-start.5 = (f32[8,128]{1,0:T(8,128)S(1)}, f32[8,128]{1,0:T(8,128)S(1)}, u32[]{:S(2)}, u32[]{:S(2)}) collective-permute-start(f32[8,128]{1,0:T(8,128)S(1)} %add_add_fusion.1), channel_id=1, source_target_pairs={{0,128},{16,144},{32,160},{48,176},{64,192},{80,208},{96,224},{112... | collective-permute-start | bytes 12296 | tf_op jit(solution)/shard_map/ppermute | solution.py:359
  90.4 17.8 %collective-permute-start.8 = (f32[8,128]{1,0:T(8,128)S(1)}, f32[8,128]{1,0:T(8,128)S(1)}, u32[]{:S(2)}, u32[]{:S(2)}) collective-permute-start(f32[8,128]{1,0:T(8,128)S(1)} %add_add_fusion), channel_id=1, source_target_pairs={{0,8},{1,9},{2,10},{3,11},{4,12},{5,13},{6,14},{7,15},{8,0},{9,1},... | collective-permute-start | bytes 12296 | tf_op jit(solution)/shard_map/ppermute | solution.py:355
  109.1 16.2 %all-to-all-start.3 = ((bf16[8,288,128]{2,1,0:T(8,128)(2,1)}), bf16[8,288,128]{2,1,0:T(8,128)(2,1)S(1)}, u32[]{:S(2)}, u32[]{:S(2)}) async-start(bf16[8,288,128]{2,1,0:T(8,128)(2,1)} %combine.1), calls=%async_computation.3 | async-start | bytes 1179648 | tf_op jit(solution)/shard_map/all_to_all | solution.py:391

commit v4 on v3

--- a/solution.py
+++ b/solution.py
@@ -112,6 +112,7 @@
     dq_t,
     gain_acc,
     first_all,
+    dscore,
     qd_ref,
     qd_sem,
     dq_out,
@@ -159,7 +160,7 @@
                 part = slice(j * rows, (j + 1) * rows)
                 k_all[at, part, :] = ref[2 * b + j, :rows, :]
                 v_all[at, part, :] = ref[2 * b + j, rows : 2 * rows, :]
-            kt_all[at] = dot(unit, k_all[at], NT).astype(BF16)
+            kt_all[:, at * size : (at + 1) * size] = dot(unit, k_all[at], NT).astype(BF16)
 
     ids_own = jnp.concatenate(
         [own_kv_ref[b, 2 * rows :, :][:1].astype(F32) for b in range(blocks)], 0
@@ -190,7 +191,7 @@
     def q_block(i, carry):
         load(i).wait()
         q_all = jnp.concatenate([part_of(i, layer, h, 0) for _, h, layer in chunks], 0)
-        q_all = dot(unit, q_all, NT)
+        q_all = q_all.astype(F32).T
         for at, h, layer in chunks:
             q = q_all[:, at]
             inv = lax.rsqrt(jnp.mean(q * q, axis=0, keepdims=True) + 1e-6)
@@ -205,7 +206,6 @@
         count = last - first + 1
         begin_int = begin_row.astype(jnp.int32)
         token = last * size + lax.broadcasted_iota(jnp.int32, (1, size), 1)
-        dq_t[...] = jnp.zeros_like(dq_t)
 
         def sums(j, n, carry):
             kb = first + j
@@ -245,20 +245,22 @@
 
             def grads(j, carry):
                 kb = first + j
-                kt = kt_all[kb]
                 probs, scores = [], []
                 for (at, _, _), (top, _, _), share, delta in zip(chunks, stats, shares, deltas):
                     prob = expo[j, :, at] * (share * jnp.exp2((tops[j, :, at] - top) * rate))
                     ds = (prob * ((dprob[j, :, at] - delta) * scale)).astype(BF16)
                     probs.append(prob.astype(BF16))
                     scores.append(ds)
-                    dq_t[:, at] += dot(kt, ds, NN)
-                acc_k[kb] += dot(jnp.concatenate(scores, 1), normed_t[...], NT)
+                ds = jnp.concatenate(scores, 1)
+                dscore[j * size : (j + 1) * size, :] = ds
+                acc_k[kb] += dot(ds, normed_t[...], NT)
                 acc_v[kb] += dot(jnp.concatenate(probs, 1), dout[...], NN)
                 return carry
 
             for j in range(n):
                 grads(j, 0)
+            cols = pl.ds(pl.multiple_of(first * size, size), n * size)
+            dq_t[...] = dot(kt_all[:, cols], dscore[: n * size, :], NN)
 
         for n in range(1, half + 2):
             pl.when(count == n)(functools.partial(run, n))
@@ -322,7 +324,7 @@
         scratch_shapes=[
             pltpu.VMEM((2 * half, size, HD), BF16),
             pltpu.VMEM((2 * half, size, HD), BF16),
-            pltpu.VMEM((2 * half, HD, size), BF16),
+            pltpu.VMEM((HD, 2 * half * size), BF16),
             pltpu.VMEM((half, 1, size), F32),
             pltpu.VMEM((HD, stack), F32),
             pltpu.VMEM((1, stack), F32),
@@ -336,6 +338,7 @@
             pltpu.VMEM((HD, stack), F32),
             pltpu.VMEM((layers, HD, rows), F32),
             pltpu.SMEM((half,), jnp.int32),
+            pltpu.VMEM(((half + 1) * size, stack), BF16),
             pltpu.VMEM((parts, twice, rows, width), BF16),
             pltpu.SemaphoreType.DMA((half,)),
             pltpu.VMEM((parts, layers, rows, width), BF16),

time: 128 us -> 128 us (level)
  starting transfers between devices: 63 us -> 66.1 us
    ppermute x1, starting transfers between devices: 16.8 us -> 19.8 us  [pair_sum(): return x + lax.ppermute(x, axis, perm)]
  transfers between devices with their start and end apart: 13 -> 13, of which waited for: 8 -> 9; matrix products, arithmetic and copies ran while one was open for 0% -> 0% of each run, Pallas kernels for 4% -> 4%
where the time goes in v4:
time: 128 us; the launch traced here: 127 us
  starting transfers between devices  66.1 us (52%)
  waiting for transfers between devices  38.9 us (30%)
  Pallas kernels  21 us (16%)
    all_to_all x4, waiting for transfers between devices, exchange(): return lax.all_to_all(x, 'sp', 0, 0, axis_index_groups=groups, tiled=True)  22.5 us
    all_to_all x4, starting transfers between devices, exchange(): return lax.all_to_all(x, 'sp', 0, 0, axis_index_groups=groups, tiled=True)  22 us
    ppermute x1, starting transfers between devices, pair_sum(): return x + lax.ppermute(x, axis, perm)  19.8 us
    ppermute x6, starting transfers between devices, ring_sum(): one, two, three = (lax.ppermute(x, axis, shift(k)) for k in (1, 2, 3))  14.9 us
    pallas_call x1, Pallas kernels, attention(): pl.pallas_call(attention_kernel, out_shape=(jax.ShapeDtypeStruct((parts,...  13.1 us
    ppermute x1, waiting for transfers between devices, on_device(): kv_low = lax.ppermute(kv_own, 'sp', low_to_up)  11.8 us
    ppermute x1, starting transfers between devices, on_device(): kv_low = lax.ppermute(kv_own, 'sp', low_to_up)  8.11 us
    ppermute x6, waiting for transfers between devices, ring_sum(): one, two, three = (lax.ppermute(x, axis, shift(k)) for k in (1, 2, 3))  3.59 us
  transfers between devices with their start and end apart: 13, of which 9 were waited for; matrix products, arithmetic and copies ran while one was open for 0% of the time, Pallas kernels for 4%

profile of v4, /device:TPU:1, one launch (start us, length us, event | category | flops | bytes accessed | tf_op | source)
XLA Modules:
  0.0 127.5 jit_solution(3641525903198396816)
XLA Ops:
  0.6 1.9 %pack_kv.1 = bf16[8,272,128]{2,1,0:T(8,128)(2,1)} custom-call(bf16[128,1024]{1,0:T(8,128)(2,1)} %bitcast.13, bf16[128,1024]{1,0:T(8,128)(2,1)} %bitcast.14, s32[1,128]{1,0:T(1,128)} %seg_ref.1), custom_call_target="tpu_custom_call" | custom-call | tf_op jit(solution)/shard_map/pack_kv/pallas_call | solution.py:396
  2.6 6.7 %all-to-all-start = ((bf16[8,272,128]{2,1,0:T(8,128)(2,1)}), bf16[8,272,128]{2,1,0:T(8,128)(2,1)S(1)}, u32[]{:S(2)}, u32[]{:S(2)}) async-start(bf16[8,272,128]{2,1,0:T(8,128)(2,1)} %pack_kv.1), calls=%async_computation | async-start | bytes 1114112 | tf_op jit(solution)/shard_map/all_to_all | solution.py:394
  9.2 3.0 %pack_q.1 = bf16[8,4,128,256]{3,2,1,0:T(8,128)(2,1)} custom-call(bf16[2,128,2048]{2,1,0:T(8,128)(2,1)} %bitcast.11, bf16[2,128,2048]{2,1,0:T(8,128)(2,1)} %bitcast.12), custom_call_target="tpu_custom_call" | custom-call | tf_op jit(solution)/shard_map/pack_q/pallas_call | solution.py:406
  12.2 6.8 %all-to-all-done.own_kv_ref = bf16[8,272,128]{2,1,0:T(8,128)(2,1)S(1)} async-done(((bf16[8,272,128]{2,1,0:T(8,128)(2,1)}), bf16[8,272,128]{2,1,0:T(8,128)(2,1)S(1)}, u32[]{:S(2)}, u32[]{:S(2)}) %all-to-all-start) | async-done | bytes 557088 | tf_op jit(solution)/shard_map/all_to_all | solution.py:394
  19.1 5.1 %all-to-all-start.1 = ((bf16[8,4,128,256]{3,2,1,0:T(8,128)(2,1)}), bf16[8,4,128,256]{3,2,1,0:T(8,128)(2,1)}, u32[]{:S(2)}, u32[]{:S(2)}) async-start(bf16[8,4,128,256]{3,2,1,0:T(8,128)(2,1)} %pack_q.1), calls=%async_computation.1 | async-start | bytes 4194304 | tf_op jit(solution)/shard_map/all_to_all | solution.py:394
  24.2 8.1 %collective-permute-start = (bf16[8,272,128]{2,1,0:T(8,128)(2,1)S(1)}, bf16[8,272,128]{2,1,0:T(8,128)(2,1)S(1)}, u32[]{:S(2)}, u32[]{:S(2)}) collective-permute-start(bf16[8,272,128]{2,1,0:T(8,128)(2,1)S(1)} %all-to-all-done.own_kv_ref), channel_id=1, source_target_pairs={{0,8},{1,9},{2,10},{3,11},{4,12},{5,13},{6,14},{7,15},{16,24},{17,... | collective-permute-start | bytes 1671176 | tf_op jit(solution)/shard_map/ppermute | solution.py:414
  32.3 11.8 %collective-permute-done.low_kv_ref = bf16[8,272,128]{2,1,0:T(8,128)(2,1)S(1)} collective-permute-done((bf16[8,272,128]{2,1,0:T(8,128)(2,1)S(1)}, bf16[8,272,128]{2,1,0:T(8,128)(2,1)S(1)}, u32[]{:S(2)}, u32[]{:S(2)}) %collective-permute-start) | collective-permute-done | bytes 557088 | tf_op jit(solution)/shard_map/ppermute | solution.py:414
  44.1 6.5 %all-to-all-done.1.qd_hbm = bf16[8,4,128,256]{3,2,1,0:T(8,128)(2,1)} async-done(((bf16[8,4,128,256]{3,2,1,0:T(8,128)(2,1)}), bf16[8,4,128,256]{3,2,1,0:T(8,128)(2,1)}, u32[]{:S(2)}, u32[]{:S(2)}) %all-to-all-start.1) | async-done | bytes 2097184 | tf_op jit(solution)/shard_map/all_to_all | solution.py:394
  50.6 13.1 %attention.1 = (bf16[8,2,128,256]{3,2,1,0:T(8,128)(2,1)}, f32[8,256,128]{2,1,0:T(8,128)}, bf16[8,256,128]{2,1,0:T(8,128)(2,1)S(1)}, f32[8,128]{1,0:T(8,128)S(1)}) custom-call(s32[1]{0:T(128)} %bitcast.upper_ref, bf16[8,272,128]{2,1,0:T(8,128)(2,1)S(1)} %all-to-all-done.own_kv_ref, bf16[8,272,128]{2,1,0:T(8,128)(2,1)S(1)} %collective-permute-done.low_kv_ref, ...), custom_call_target="tpu_custom_call" | custom-call | tf_op jit(solution)/shard_map/attention/pallas_call | solution.py:314
  63.8 0.8 copy-done.2
  64.6 4.5 %all-to-all-start.2 = ((bf16[8,2,128,256]{3,2,1,0:T(8,128)(2,1)}), bf16[8,2,128,256]{3,2,1,0:T(8,128)(2,1)S(1)}, u32[]{:S(2)}, u32[]{:S(2)}) async-start(bf16[8,2,128,256]{3,2,1,0:T(8,128)(2,1)} %get-tuple-element.15), calls=%async_computation.2 | async-start | bytes 2097152 | tf_op jit(solution)/shard_map/all_to_all | solution.py:394
  69.1 1.3 %collective-permute-start.1 = (bf16[8,256,128]{2,1,0:T(8,128)(2,1)S(1)}, bf16[8,256,128]{2,1,0:T(8,128)(2,1)S(1)}, u32[]{:S(2)}, u32[]{:S(2)}) collective-permute-start(bf16[8,256,128]{2,1,0:T(8,128)(2,1)S(1)} %copy-done.3), channel_id=1, source_target_pairs={{8,0},{9,1},{10,2},{11,3},{12,4},{13,5},{14,6},{15,7},{24,16},{25,... | collective-permute-start | bytes 1572872 | tf_op jit(solution)/shard_map/ppermute | solution.py:419
  70.3 1.8 %collective-permute-start.4 = (f32[8,128]{1,0:T(8,128)S(1)}, f32[8,128]{1,0:T(8,128)S(1)}, u32[]{:S(2)}, u32[]{:S(2)}) collective-permute-start(f32[8,128]{1,0:T(8,128)S(1)} %get-tuple-element.18), channel_id=1, source_target_pairs={{0,48},{16,0},{32,16},{48,32},{64,112},{80,64},{96,80},{112,96},{1... | collective-permute-start | bytes 12296 | tf_op jit(solution)/shard_map/ppermute | solution.py:362
  72.2 0.0 collective-permute-start.3
  72.2 4.4 %collective-permute-start.2 = (f32[8,128]{1,0:T(8,128)S(1)}, f32[8,128]{1,0:T(8,128)S(1)}, u32[]{:S(2)}, u32[]{:S(2)}) collective-permute-start(f32[8,128]{1,0:T(8,128)S(1)} %get-tuple-element.18), channel_id=1, source_target_pairs={{0,32},{16,48},{32,0},{48,16},{64,96},{80,112},{96,64},{112,80},{1... | collective-permute-start | bytes 12296 | tf_op jit(solution)/shard_map/ppermute | solution.py:362
  76.6 0.0 collective-permute-done.4
  76.6 0.0 collective-permute-done.3
  76.6 1.0 collective-permute-done.2
  77.7 5.6 %collective-permute-start.7 = (f32[8,128]{1,0:T(8,128)S(1)}, f32[8,128]{1,0:T(8,128)S(1)}, u32[]{:S(2)}, u32[]{:S(2)}) collective-permute-start(f32[8,128]{1,0:T(8,128)S(1)} %add_add_fusion.1), channel_id=1, source_target_pairs={{0,192},{16,208},{32,224},{48,240},{64,0},{80,16},{96,32},{112,48}... | collective-permute-start | bytes 12296 | tf_op jit(solution)/shard_map/ppermute | solution.py:362
  83.3 1.9 %collective-permute-start.6 = (f32[8,128]{1,0:T(8,128)S(1)}, f32[8,128]{1,0:T(8,128)S(1)}, u32[]{:S(2)}, u32[]{:S(2)}) collective-permute-start(f32[8,128]{1,0:T(8,128)S(1)} %add_add_fusion.1), channel_id=1, source_target_pairs={{0,64},{16,80},{32,96},{48,112},{64,128},{80,144},{96,160},{112,17... | collective-permute-start | bytes 12296 | tf_op jit(solution)/shard_map/ppermute | solution.py:362
  85.2 1.1 collective-permute-start.5
  86.3 0.1 collective-permute-done.7
  86.4 1.4 %collective-permute-done.6 = f32[8,128]{1,0:T(8,128)S(1)} collective-permute-done((f32[8,128]{1,0:T(8,128)S(1)}, f32[8,128]{1,0:T(8,128)S(1)}, u32[]{:S(2)}, u32[]{:S(2)}) %collective-permute-start.6) | collective-permute-done | bytes 4128 | tf_op jit(solution)/shard_map/ppermute | solution.py:362
  87.8 1.0 collective-permute-done.5
  88.9 19.8 %collective-permute-start.8 = (f32[8,128]{1,0:T(8,128)S(1)}, f32[8,128]{1,0:T(8,128)S(1)}, u32[]{:S(2)}, u32[]{:S(2)}) collective-permute-start(f32[8,128]{1,0:T(8,128)S(1)} %add_add_fusion), channel_id=1, source_target_pairs={{0,8},{1,9},{2,10},{3,11},{4,12},{5,13},{6,14},{7,15},{8,0},{9,1},... | collective-permute-start | bytes 12296 | tf_op jit(solution)/shard_map/ppermute | solution.py:358
  108.7 1.0 collective-permute-done.8
  109.7 0.0 collective-permute-done.1.cross_ref
  109.7 0.9 combine.1
  110.6 5.7 %all-to-all-start.3 = ((bf16[8,288,128]{2,1,0:T(8,128)(2,1)}), bf16[8,288,128]{2,1,0:T(8,128)(2,1)S(1)}, u32[]{:S(2)}, u32[]{:S(2)}) async-start(bf16[8,288,128]{2,1,0:T(8,128)(2,1)} %combine.1), calls=%async_computation.3 | async-start | bytes 1179648 | tf_op jit(solution)/shard_map/all_to_all | solution.py:394
  116.4 1.1 unpack_q.1
  117.5 9.1 %all-to-all-done.3.in_ref = bf16[8,288,128]{2,1,0:T(8,128)(2,1)S(1)} async-done(((bf16[8,288,128]{2,1,0:T(8,128)(2,1)}), bf16[8,288,128]{2,1,0:T(8,128)(2,1)S(1)}, u32[]{:S(2)}, u32[]{:S(2)}) %all-to-all-start.3) | async-done | bytes 589856 | tf_op jit(solution)/shard_map/all_to_all | solution.py:394
  126.6 0.9 unpack_kv.1
  (11 shorter events, 0.0 us)
Async XLA Ops:
  2.6 16.5 %all-to-all-start = ((bf16[8,272,128]{2,1,0:T(8,128)(2,1)}), bf16[8,272,128]{2,1,0:T(8,128)(2,1)S(1)}, u32[]{:S(2)}, u32[]{:S(2)}) async-start(bf16[8,272,128]{2,1,0:T(8,128)(2,1)} %pack_kv.1), calls=%async_computation | async-start | bytes 1114112 | tf_op jit(solution)/shard_map/all_to_all | solution.py:394
  12.2 38.4 %copy-start.1 = (f32[2,128]{1,0:T(2,128)S(1)}, f32[2,128]{1,0:T(2,128)}, u32[]{:S(2)}) copy-start(f32[2,128]{1,0:T(2,128)} %gain_ref.1) | copy-start | bytes 3076
  19.1 31.5 %all-to-all-start.1 = ((bf16[8,4,128,256]{3,2,1,0:T(8,128)(2,1)}), bf16[8,4,128,256]{3,2,1,0:T(8,128)(2,1)}, u32[]{:S(2)}, u32[]{:S(2)}) async-start(bf16[8,4,128,256]{3,2,1,0:T(8,128)(2,1)} %pack_q.1), calls=%async_computation.1 | async-start | bytes 4194304 | tf_op jit(solution)/shard_map/all_to_all | solution.py:394
  24.2 19.9 %collective-permute-start = (bf16[8,272,128]{2,1,0:T(8,128)(2,1)S(1)}, bf16[8,272,128]{2,1,0:T(8,128)(2,1)S(1)}, u32[]{:S(2)}, u32[]{:S(2)}) collective-permute-start(bf16[8,272,128]{2,1,0:T(8,128)(2,1)S(1)} %all-to-all-done.own_kv_ref), channel_id=1, source_target_pairs={{0,8},{1,9},{2,10},{3,11},{4,12},{5,13},{6,14},{7,15},{16,24},{17,... | collective-permute-start | bytes 1671176 | tf_op jit(solution)/shard_map/ppermute | solution.py:414
  63.8 0.8 copy-start.2
  64.6 45.1 %copy-start = (f32[8,256,128]{2,1,0:T(8,128)S(1)}, f32[8,256,128]{2,1,0:T(8,128)}, u32[]{:S(2)}) copy-start(f32[8,256,128]{2,1,0:T(8,128)} %get-tuple-element.16.own_ref) | copy-start | bytes 3145732
  64.6 4.5 %copy-start.3 = (bf16[8,256,128]{2,1,0:T(8,128)(2,1)S(1)}, bf16[8,256,128]{2,1,0:T(8,128)(2,1)}, u32[]{:S(2)}) copy-start(bf16[8,256,128]{2,1,0:T(8,128)(2,1)} %copy-done.2) | copy-start | bytes 1572868
  64.6 46.0 %all-to-all-start.2 = ((bf16[8,2,128,256]{3,2,1,0:T(8,128)(2,1)}), bf16[8,2,128,256]{3,2,1,0:T(8,128)(2,1)S(1)}, u32[]{:S(2)}, u32[]{:S(2)}) async-start(bf16[8,2,128,256]{3,2,1,0:T(8,128)(2,1)} %get-tuple-element.15), calls=%async_computation.2 | async-start | bytes 2097152 | tf_op jit(solution)/shard_map/all_to_all | solution.py:394
  69.1 40.6 %collective-permute-start.1 = (bf16[8,256,128]{2,1,0:T(8,128)(2,1)S(1)}, bf16[8,256,128]{2,1,0:T(8,128)(2,1)S(1)}, u32[]{:S(2)}, u32[]{:S(2)}) collective-permute-start(bf16[8,256,128]{2,1,0:T(8,128)(2,1)S(1)} %copy-done.3), channel_id=1, source_target_pairs={{8,0},{9,1},{10,2},{11,3},{12,4},{13,5},{14,6},{15,7},{24,16},{25,... | collective-permute-start | bytes 1572872 | tf_op jit(solution)/shard_map/ppermute | solution.py:419
  70.3 6.3 %collective-permute-start.4 = (f32[8,128]{1,0:T(8,128)S(1)}, f32[8,128]{1,0:T(8,128)S(1)}, u32[]{:S(2)}, u32[]{:S(2)}) collective-permute-start(f32[8,128]{1,0:T(8,128)S(1)} %get-tuple-element.18), channel_id=1, source_target_pairs={{0,48},{16,0},{32,16},{48,32},{64,112},{80,64},{96,80},{112,96},{1... | collective-permute-start | bytes 12296 | tf_op jit(solution)/shard_map/ppermute | solution.py:362
  72.2 4.4 %collective-permute-start.3 = (f32[8,128]{1,0:T(8,128)S(1)}, f32[8,128]{1,0:T(8,128)S(1)}, u32[]{:S(2)}, u32[]{:S(2)}) collective-permute-start(f32[8,128]{1,0:T(8,128)S(1)} %get-tuple-element.18), channel_id=1, source_target_pairs={{0,16},{16,32},{32,48},{48,0},{64,80},{80,96},{96,112},{112,64},{1... | collective-permute-start | bytes 12296 | tf_op jit(solution)/shard_map/ppermute | solution.py:362
  72.2 5.5 %collective-permute-start.2 = (f32[8,128]{1,0:T(8,128)S(1)}, f32[8,128]{1,0:T(8,128)S(1)}, u32[]{:S(2)}, u32[]{:S(2)}) collective-permute-start(f32[8,128]{1,0:T(8,128)S(1)} %get-tuple-element.18), channel_id=1, source_target_pairs={{0,32},{16,48},{32,0},{48,16},{64,96},{80,112},{96,64},{112,80},{1... | collective-permute-start | bytes 12296 | tf_op jit(solution)/shard_map/ppermute | solution.py:362
  77.7 8.7 %collective-permute-start.7 = (f32[8,128]{1,0:T(8,128)S(1)}, f32[8,128]{1,0:T(8,128)S(1)}, u32[]{:S(2)}, u32[]{:S(2)}) collective-permute-start(f32[8,128]{1,0:T(8,128)S(1)} %add_add_fusion.1), channel_id=1, source_target_pairs={{0,192},{16,208},{32,224},{48,240},{64,0},{80,16},{96,32},{112,48}... | collective-permute-start | bytes 12296 | tf_op jit(solution)/shard_map/ppermute | solution.py:362
  83.3 4.6 %collective-permute-start.6 = (f32[8,128]{1,0:T(8,128)S(1)}, f32[8,128]{1,0:T(8,128)S(1)}, u32[]{:S(2)}, u32[]{:S(2)}) collective-permute-start(f32[8,128]{1,0:T(8,128)S(1)} %add_add_fusion.1), channel_id=1, source_target_pairs={{0,64},{16,80},{32,96},{48,112},{64,128},{80,144},{96,160},{112,17... | collective-permute-start | bytes 12296 | tf_op jit(solution)/shard_map/ppermute | solution.py:362
  85.2 3.7 %collective-permute-start.5 = (f32[8,128]{1,0:T(8,128)S(1)}, f32[8,128]{1,0:T(8,128)S(1)}, u32[]{:S(2)}, u32[]{:S(2)}) collective-permute-start(f32[8,128]{1,0:T(8,128)S(1)} %add_add_fusion.1), channel_id=1, source_target_pairs={{0,128},{16,144},{32,160},{48,176},{64,192},{80,208},{96,224},{112... | collective-permute-start | bytes 12296 | tf_op jit(solution)/shard_map/ppermute | solution.py:362
  88.9 20.8 %collective-permute-start.8 = (f32[8,128]{1,0:T(8,128)S(1)}, f32[8,128]{1,0:T(8,128)S(1)}, u32[]{:S(2)}, u32[]{:S(2)}) collective-permute-start(f32[8,128]{1,0:T(8,128)S(1)} %add_add_fusion), channel_id=1, source_target_pairs={{0,8},{1,9},{2,10},{3,11},{4,12},{5,13},{6,14},{7,15},{8,0},{9,1},... | collective-permute-start | bytes 12296 | tf_op jit(solution)/shard_map/ppermute | solution.py:358
  110.6 15.9 %all-to-all-start.3 = ((bf16[8,288,128]{2,1,0:T(8,128)(2,1)}), bf16[8,288,128]{2,1,0:T(8,128)(2,1)S(1)}, u32[]{:S(2)}, u32[]{:S(2)}) async-start(bf16[8,288,128]{2,1,0:T(8,128)(2,1)} %combine.1), calls=%async_computation.3 | async-start | bytes 1179648 | tf_op jit(solution)/shard_map/all_to_all | solution.py:394
